TPU v7x, 256 devices: a whole 4x4x8 slice. The times are simulated.
256 devices in a mesh: enc: 8 (over y, core), seq: 32 (over z, x).
Axes of the slice: x: 4, y: 4, z: 8, core: 2. Of those that a mesh axis runs over, the one named last changes fastest.
Arguments:
- patches: bfloat16 [32, 896, 1280], P('seq', 'enc'), may hold values from -6 to 6
- vision_gain: float32 [1280], replicated, may hold values from 0.2 to 3
- merge_up: bfloat16 [5120, 2560], P(None, 'enc'), may hold values from -0.078125 to 0.078125
- merge_up_bias: float32 [2560], P('enc'), may hold values from -3 to 3
- merge_down: bfloat16 [2560, 4096], P('enc'), may hold values from -0.15625 to 0.15625
- merge_down_bias: float32 [4096], P('enc'), may hold values from -3 to 3
- text_embed: bfloat16 [8192, 4096], P('seq', 'enc'), may hold values from -6 to 6
- image_lengths: int32 [32, 16], replicated, may hold values from 1 to 16, as said below
- image_offsets: int32 [32, 16], replicated, may hold values from 0 to 8191, as said below
- input_gain: float32 [4096], replicated, may hold values from 0.1 to 1.9
- qkv_weight: bfloat16 [4096, 5120], P(None, 'enc'), may hold values from -0.09375 to 0.09375
- qkv_bias: float32 [5120], P('enc'), may hold values from -24 to 24
Outputs:
- attention: bfloat16 [8192, 4096], P('seq', 'enc')
Inputs may be any that keep to these rules, and one draw needn't show every extreme that they name: `image_lengths`: each row sums to 224; every row has a frame of exactly 16 merged tokens. `image_offsets`: A frame's tokens are consecutive and lie within one sequence shard of 256 tokens; no two frames share a token. The 16 frames of one group go to 16 different shards, and every shard receives 16 frames, each from a different group.
All inputs are finite; a program needn't handle non-finite values.
Results may differ from a plain program's by a relative error of at most 0.025.
Values may be sent and summed in bfloat16 or wider, within the bound.
A program may use at most 64 MiB of HBM per device.

v0:
```python
import math

import jax
import jax.numpy as jnp
from jax import lax
from jax.sharding import PartitionSpec as P

HD = 128
HEADS_DEV = 4
LMAX = 16


EPSILON = 1e-06
THETA = 1000000.0


def from_partner(block, axis, stride):
    count = lax.axis_size(axis)
    route = []
    for low in range(count):
        high = low | 1 << stride
        if high != low and high < count:
            route += [(low, high), (high, low)]
    return lax.ppermute(block, axis, route)


def rms_norm(values, scale_gain):
    widened = values.astype(jnp.float32)
    mean_square = jnp.mean(widened * widened, axis=-1, keepdims=True)
    return widened * lax.rsqrt(mean_square + EPSILON) * scale_gain


def rotate(values, positions):
    half_dim = values.shape[-1] // 2
    steps_f = jnp.arange(half_dim).astype(jnp.float32)
    inv_freq = jnp.exp(steps_f * (-2.0 * jnp.log(THETA) / values.shape[-1]))
    angles = positions[:, None] * inv_freq[None, :]
    cosine = jnp.cos(angles)[:, None, :]
    sine_part = jnp.sin(angles)[:, None, :]
    first_half = values[..., :half_dim]
    second_half = values[..., half_dim:]
    return jnp.concatenate(
        [
            first_half * cosine - second_half * sine_part,
            second_half * cosine + first_half * sine_part,
        ],
        axis=-1,
    )


def local(
    patches,
    vision_gain,
    merge_up,
    merge_up_bias,
    merge_down,
    merge_down_bias,
    text_embed,
    image_lengths,
    image_offsets,
    input_gain,
    qkv_weight,
    qkv_bias,
):
    seq_count = lax.axis_size("seq")
    seq_index = lax.axis_index("seq")
    enc_index = lax.axis_index("enc")
    tok_rows = text_embed.shape[0]
    normed = rms_norm(patches[0], vision_gain).astype(jnp.bfloat16)
    grouped = normed.reshape(normed.shape[0] // 4, 4 * normed.shape[1])
    inner = jax.nn.gelu(
        jnp.dot(
            lax.all_gather(grouped, "enc", axis=0, tiled=True),
            merge_up,
            preferred_element_type=jnp.float32,
        )
        + merge_up_bias,
        approximate=False,
    ).astype(jnp.bfloat16)
    shares = jnp.dot(inner, merge_down, preferred_element_type=jnp.float32)
    embeddings = (
        lax.psum_scatter(
            shares.astype(jnp.bfloat16), "enc", scatter_dimension=1, tiled=True
        ).astype(jnp.float32)
        + merge_down_bias
    ).astype(jnp.bfloat16)
    slot_ids = jnp.arange(LMAX, dtype=jnp.int32)
    peer_ids = jnp.arange(seq_count, dtype=jnp.int32)
    my_lengths = lax.dynamic_index_in_dim(image_lengths, seq_index, 0, keepdims=False)
    my_offsets = lax.dynamic_index_in_dim(image_offsets, seq_index, 0, keepdims=False)
    my_starts = jnp.cumsum(my_lengths) - my_lengths
    to_peer = (my_offsets // tok_rows)[None, :] == peer_ids[:, None]
    peer_start = jnp.sum(jnp.where(to_peer, my_starts[None, :], 0), axis=1)
    peer_length = jnp.sum(jnp.where(to_peer, my_lengths[None, :], 0), axis=1)
    filled = slot_ids[None, :] < peer_length[:, None]
    row_index = jnp.where(filled, peer_start[:, None] + slot_ids[None, :], 0)
    picked = jnp.take(embeddings, row_index.reshape(-1), axis=0).reshape(
        seq_count, LMAX, embeddings.shape[1]
    )
    outgoing = jnp.where(filled[:, :, None], picked, jnp.zeros_like(picked))
    incoming = lax.all_to_all(outgoing, "seq", split_axis=0, concat_axis=0, tiled=True)
    from_peer = image_offsets // tok_rows == seq_index
    peer_offset = jnp.sum(jnp.where(from_peer, image_offsets, 0), axis=1) - seq_index * tok_rows
    peer_count = jnp.sum(jnp.where(from_peer, image_lengths, 0), axis=1)
    arriving = slot_ids[None, :] < peer_count[:, None]
    target = jnp.where(arriving, peer_offset[:, None] + slot_ids[None, :], tok_rows)
    local_tokens = text_embed.at[target.reshape(-1)].set(
        incoming.reshape(-1, incoming.shape[-1]), mode="drop"
    )
    full_rows = lax.all_gather(local_tokens, "enc", axis=1, tiled=True)
    normed_tokens = rms_norm(full_rows, input_gain).astype(jnp.bfloat16)
    projected = jnp.dot(normed_tokens, qkv_weight, preferred_element_type=jnp.float32) + qkv_bias
    token_ids = seq_index * tok_rows + jnp.arange(tok_rows, dtype=jnp.int32)
    positions = token_ids.astype(jnp.float32)
    query_width = HEADS_DEV * HD
    queries = rotate(projected[:, :query_width].reshape(tok_rows, HEADS_DEV, HD), positions)
    kv_part = projected[:, query_width:]
    is_key = enc_index % 2 == 0
    rotated = rotate(kv_part[:, None, :], positions)[:, 0, :]
    rounded = lax.optimization_barrier(kv_part.astype(jnp.bfloat16)).astype(jnp.float32)
    kv_part = jnp.where(is_key, rotated, rounded)
    query_rows = queries.reshape(tok_rows * HEADS_DEV, HD)
    query_pos = jnp.repeat(token_ids, HEADS_DEV)
    score_scale = HD ** (-0.5)
    row_count = query_rows.shape[0]
    initial = (
        jnp.full((row_count,), -1e30, jnp.float32),
        jnp.zeros((row_count,), jnp.float32),
        jnp.zeros((row_count, HD), jnp.float32),
    )
    partner = from_partner(kv_part, "enc", 0)
    key_rows = jnp.where(is_key, kv_part, partner)
    value_rows = jnp.where(is_key, partner, kv_part)
    key_piece = lax.all_gather(key_rows, "seq", axis=0, tiled=True)
    value_piece = lax.all_gather(value_rows, "seq", axis=0, tiled=True)
    piece_rows = key_piece.shape[0]
    block_rows = math.gcd(piece_rows, 1024)
    block_count = piece_rows // block_rows
    key_blocks = key_piece.reshape(block_count, block_rows, HD)
    value_blocks = value_piece.reshape(block_count, block_rows, HD)

    def block_step(state_now, inputs):
        block_id, key_block, value_block = inputs
        old_max, old_sum, old_acc = state_now
        scores = (
            jnp.einsum(
                "qd,kd->qk",
                query_rows,
                key_block,
                preferred_element_type=jnp.float32,
                precision=lax.Precision.HIGHEST,
            )
            * score_scale
        )
        key_pos = block_id * block_rows + jnp.arange(block_rows, dtype=jnp.int32)
        allowed = key_pos[None, :] <= query_pos[:, None]
        new_max = jnp.maximum(old_max, jnp.max(jnp.where(allowed, scores, -1e30), axis=1))
        weights = jnp.where(allowed, jnp.exp(scores - new_max[:, None]), 0.0)
        factor = jnp.exp(old_max - new_max)
        new_sum = old_sum * factor + jnp.sum(weights, axis=1)
        new_acc = old_acc * factor[:, None] + jnp.dot(
            weights.astype(jnp.bfloat16),
            value_block.astype(jnp.bfloat16),
            preferred_element_type=jnp.float32,
        )
        return ((new_max, new_sum, new_acc), None)

    final_state, _ = lax.scan(
        block_step, initial, (jnp.arange(block_count, dtype=jnp.int32), key_blocks, value_blocks)
    )
    run_max, run_sum, run_acc = final_state
    attended = (run_acc / run_sum[:, None]).astype(jnp.bfloat16)
    return attended.reshape(tok_rows, HEADS_DEV * HD)


def solution(mesh):
    in_specs = (
        P("seq", "enc", None),
        P(),
        P(None, "enc"),
        P("enc"),
        P("enc", None),
        P("enc"),
        P("seq", "enc"),
        P(),
        P(),
        P(),
        P(None, "enc"),
        P("enc"),
    )
    out_specs = P("seq", "enc")
    return jax.shard_map(local, mesh=mesh, in_specs=in_specs, out_specs=out_specs, check_vma=False)
```

profile of v0, /device:TPU:249, one launch (start us, length us, event | category | flops | bytes accessed | tf_op | source)
XLA Modules:
  0.0 444.8 jit_solution(1720026595232235710)
XLA Ops:
  13.3 28.4 %all-gather.12.cloned.1.call-done = bf16[8,28,5120]{2,1,0:T(8,128)(2,1)} async-done(((bf16[1,28,5120]{2,1,0:T(8,128)(2,1)}), bf16[8,28,5120]{2,1,0:T(8,128)(2,1)}) %all-gather.12.cloned.1.call-update) | async-done | bytes 2293776 | tf_op jit(solution)/shard_map/all_gather | solution.py:73
  41.7 4.1 reshape.354
  45.8 8.2 %convolution_convert_fusion = bf16[224,4096]{1,0:T(8,128)(2,1)} fusion(bf16[320,4096]{1,0:T(8,128)(2,1)} %param.18, bf16[224,5120]{1,0:T(8,128)(2,1)} %reshape.354, bf16[5120,320]{0,1:T(8,128)(2,1)S(1)} %copy-done, f32[320]{0:T(512)S(1)} %copy-done.11), kind=kOutput, calls=%fused_computation.30 | convolution fusion | flops 1326854144 | bytes 10028288 | tf_op jit(solution)/shard_map/dot_general | solution.py:80
  56.2 33.0 %reduce-scatter.2.cloned.1.call-done = bf16[224,512]{1,0:T(8,128)(2,1)} async-done(((bf16[224,4096]{1,0:T(8,128)(2,1)}), bf16[224,512]{1,0:T(8,128)(2,1)}) %reduce-scatter.2.cloned.1.call-update) | async-done | bytes 229392 | tf_op jit(solution)/shard_map/reduce_scatter | solution.py:82
  95.0 9.1 %all-to-all-start = ((bf16[32,16,512]{2,1,0:T(8,128)(2,1)}), bf16[32,16,512]{2,1,0:T(8,128)(2,1)}, u32[]{:S(2)}, u32[]{:S(2)}) async-start(bf16[32,16,512]{2,1,0:T(8,128)(2,1)} %select_select_fusion), calls=%async_computation.1 | async-start | bytes 1048576 | tf_op jit(solution)/shard_map/all_to_all | solution.py:101
  105.6 13.3 %all-to-all-done = bf16[32,16,512]{2,1,0:T(8,128)(2,1)} async-done(((bf16[32,16,512]{2,1,0:T(8,128)(2,1)}), bf16[32,16,512]{2,1,0:T(8,128)(2,1)}, u32[]{:S(2)}, u32[]{:S(2)}) %all-to-all-start) | async-done | bytes 524320 | tf_op jit(solution)/shard_map/all_to_all | solution.py:101
  122.7 26.3 %all-gather.6.cloned.1.call-done = bf16[256,4096]{1,0:T(8,128)(2,1)} async-done(((bf16[256,512]{1,0:T(8,128)(2,1)}), bf16[256,4096]{1,0:T(8,128)(2,1)}) %all-gather.6.cloned.1.call-update) | async-done | bytes 2097168 | tf_op jit(solution)/shard_map/all_gather | solution.py:110
  151.1 5.0 %fusion.29 = f32[256,640]{1,0:T(8,128)S(1)} fusion(bf16[4096,640]{1,0:T(8,128)(2,1)} %param.24, bf16[256,4096]{1,0:T(8,128)(2,1)} %all-gather.6.cloned.1.call-done, f32[4096]{0:T(1024)} %param.23, f32[256]{0:T(256)S(1)} %add_rsqrt_fusion, f32[640]{0:T(1024)S(1)} %copy-done.10), kind=kOutput, calls=%fused_computation.37 | convolution fusion | flops 1346535424 | bytes 8015360 | tf_op jit(solution)/shard_map/dot_general | solution.py:112
  167.7 65.2 %all-gather.10.cloned.1.call-done = bf16[8192,128]{1,0:T(8,128)(2,1)} async-done(((bf16[256,128]{1,0:T(8,128)(2,1)}), bf16[8192,128]{1,0:T(8,128)(2,1)}) %all-gather.10.cloned.1.call-update) | async-done | bytes 2097168 | tf_op jit(solution)/shard_map/all_gather | solution.py:135
  232.9 82.5 %all-gather.8.cloned.1.call-done = f32[8192,128]{1,0:T(8,128)} async-done(((f32[256,128]{1,0:T(8,128)}), f32[8192,128]{1,0:T(8,128)}) %all-gather.8.cloned.1.call-update) | async-done | bytes 4194320 | tf_op jit(solution)/shard_map/all_gather | solution.py:134
  315.4 120.7 %while.15 = (s32[]{:T(128)}, f32[1024]{0:T(1024)S(1)}, f32[1024]{0:T(1024)S(1)}, f32[1024,128]{1,0:T(8,128)}, s32[8]{0:T(128)S(1)}, /*index=5*/f32[8,1024,128]{2...) while((s32[]{:T(128)}, f32[1024]{0:T(1024)S(1)}, ...), condition=%wide.region_12.13_spmd.clone, body=%wide.region_9.12_spmd.clone.sunk | while | flops 1894127616 | bytes 31828152 | solution.py:168
  316.8 7.0 %fusion.133 = (f32[1024]{0:T(1024)S(1)}, f32[1024,1024]{1,0:T(8,128)}) fusion(s32[1024]{0:T(1024)S(1)} %le.79, s32[1024]{0:T(1024)S(1)} %iota_add_fusion.3, f32[1024,128]{1,0:T(8,128)} %get-tuple-element.217, f32[8,1024,128]{2,1,0:T(8,128)} %get-tuple-element.216, s32[]{:T(128)} %get-tuple-element.199), kind=kOutput, calls=%fused_computation.5.clone.1 | convolution fusion | flops 1614806016 | bytes 5255680 | tf_op jit(solution)/shard_map/while/body/eval_jaxpr/qd,kd->qk/dot_general | solution.py:146
  323.9 3.3 fusion.134
  331.8 7.0 %fusion.133 = (f32[1024]{0:T(1024)S(1)}, f32[1024,1024]{1,0:T(8,128)}) fusion(s32[1024]{0:T(1024)S(1)} %le.79, s32[1024]{0:T(1024)S(1)} %iota_add_fusion.3, f32[1024,128]{1,0:T(8,128)} %get-tuple-element.217, f32[8,1024,128]{2,1,0:T(8,128)} %get-tuple-element.216, s32[]{:T(128)} %get-tuple-element.199), kind=kOutput, calls=%fused_computation.5.clone.1 | convolution fusion | flops 1614806016 | bytes 5255680 | tf_op jit(solution)/shard_map/while/body/eval_jaxpr/qd,kd->qk/dot_general | solution.py:146
  338.8 3.3 fusion.134
  342.2 3.2 fusion.136
  346.9 7.0 %fusion.133 = (f32[1024]{0:T(1024)S(1)}, f32[1024,1024]{1,0:T(8,128)}) fusion(s32[1024]{0:T(1024)S(1)} %le.79, s32[1024]{0:T(1024)S(1)} %iota_add_fusion.3, f32[1024,128]{1,0:T(8,128)} %get-tuple-element.217, f32[8,1024,128]{2,1,0:T(8,128)} %get-tuple-element.216, s32[]{:T(128)} %get-tuple-element.199), kind=kOutput, calls=%fused_computation.5.clone.1 | convolution fusion | flops 1614806016 | bytes 5255680 | tf_op jit(solution)/shard_map/while/body/eval_jaxpr/qd,kd->qk/dot_general | solution.py:146
  353.9 3.3 fusion.134
  362.0 7.0 %fusion.133 = (f32[1024]{0:T(1024)S(1)}, f32[1024,1024]{1,0:T(8,128)}) fusion(s32[1024]{0:T(1024)S(1)} %le.79, s32[1024]{0:T(1024)S(1)} %iota_add_fusion.3, f32[1024,128]{1,0:T(8,128)} %get-tuple-element.217, f32[8,1024,128]{2,1,0:T(8,128)} %get-tuple-element.216, s32[]{:T(128)} %get-tuple-element.199), kind=kOutput, calls=%fused_computation.5.clone.1 | convolution fusion | flops 1614806016 | bytes 5255680 | tf_op jit(solution)/shard_map/while/body/eval_jaxpr/qd,kd->qk/dot_general | solution.py:146
  369.0 3.3 fusion.134
  372.5 3.2 fusion.136
  377.1 7.0 %fusion.133 = (f32[1024]{0:T(1024)S(1)}, f32[1024,1024]{1,0:T(8,128)}) fusion(s32[1024]{0:T(1024)S(1)} %le.79, s32[1024]{0:T(1024)S(1)} %iota_add_fusion.3, f32[1024,128]{1,0:T(8,128)} %get-tuple-element.217, f32[8,1024,128]{2,1,0:T(8,128)} %get-tuple-element.216, s32[]{:T(128)} %get-tuple-element.199), kind=kOutput, calls=%fused_computation.5.clone.1 | convolution fusion | flops 1614806016 | bytes 5255680 | tf_op jit(solution)/shard_map/while/body/eval_jaxpr/qd,kd->qk/dot_general | solution.py:146
  384.1 3.3 fusion.134
  392.2 7.0 %fusion.133 = (f32[1024]{0:T(1024)S(1)}, f32[1024,1024]{1,0:T(8,128)}) fusion(s32[1024]{0:T(1024)S(1)} %le.79, s32[1024]{0:T(1024)S(1)} %iota_add_fusion.3, f32[1024,128]{1,0:T(8,128)} %get-tuple-element.217, f32[8,1024,128]{2,1,0:T(8,128)} %get-tuple-element.216, s32[]{:T(128)} %get-tuple-element.199), kind=kOutput, calls=%fused_computation.5.clone.1 | convolution fusion | flops 1614806016 | bytes 5255680 | tf_op jit(solution)/shard_map/while/body/eval_jaxpr/qd,kd->qk/dot_general | solution.py:146
  399.2 3.3 fusion.134
  402.7 3.2 fusion.136
  407.4 7.0 %fusion.133 = (f32[1024]{0:T(1024)S(1)}, f32[1024,1024]{1,0:T(8,128)}) fusion(s32[1024]{0:T(1024)S(1)} %le.79, s32[1024]{0:T(1024)S(1)} %iota_add_fusion.3, f32[1024,128]{1,0:T(8,128)} %get-tuple-element.217, f32[8,1024,128]{2,1,0:T(8,128)} %get-tuple-element.216, s32[]{:T(128)} %get-tuple-element.199), kind=kOutput, calls=%fused_computation.5.clone.1 | convolution fusion | flops 1614806016 | bytes 5255680 | tf_op jit(solution)/shard_map/while/body/eval_jaxpr/qd,kd->qk/dot_general | solution.py:146
  414.4 3.3 fusion.134
  417.8 3.2 fusion.136
  422.5 7.0 %fusion.133 = (f32[1024]{0:T(1024)S(1)}, f32[1024,1024]{1,0:T(8,128)}) fusion(s32[1024]{0:T(1024)S(1)} %le.79, s32[1024]{0:T(1024)S(1)} %iota_add_fusion.3, f32[1024,128]{1,0:T(8,128)} %get-tuple-element.217, f32[8,1024,128]{2,1,0:T(8,128)} %get-tuple-element.216, s32[]{:T(128)} %get-tuple-element.199), kind=kOutput, calls=%fused_computation.5.clone.1 | convolution fusion | flops 1614806016 | bytes 5255680 | tf_op jit(solution)/shard_map/while/body/eval_jaxpr/qd,kd->qk/dot_general | solution.py:146
  429.5 3.3 fusion.134
  432.9 3.2 fusion.136
  (163 shorter events, 52.3 us)
Async XLA Ops:
  6.5 39.3 %copy-start = (bf16[5120,320]{0,1:T(8,128)(2,1)S(1)}, bf16[5120,320]{0,1:T(8,128)(2,1)}, u32[]{:S(2)}) copy-start(bf16[5120,320]{0,1:T(8,128)(2,1)} %param.16) | copy-start | bytes 9830404
  6.5 4.6 %copy-start.7 = (f32[1280]{0:T(1024)S(1)}, f32[1280]{0:T(1024)}, u32[]{:S(2)}) copy-start(f32[1280]{0:T(1024)} %param.15) | copy-start | bytes 15364
  6.5 35.1 %all-gather.12.cloned.1.call-start = ((), (), s32[]{:S(2)}) async-start(), calls=%async_computation.6 | async-start | bytes 2949120 | tf_op jit(solution)/shard_map/all_gather | solution.py:73
  10.2 35.6 %copy-start.11 = (f32[320]{0:T(512)S(1)}, f32[320]{0:T(512)}, u32[]{:S(2)}) copy-start(f32[320]{0:T(512)} %param.17) | copy-start | bytes 3844
  13.3 76.0 %reduce-scatter.2.cloned.1.call-start = ((), (), s32[]{:S(2)}) async-start(), calls=%async_computation.2 | async-start | bytes 2064384 | tf_op jit(solution)/shard_map/reduce_scatter | solution.py:82
  45.8 8.3 %copy-start.5 = (s32[32,16]{0,1:T(8,128)S(1)}, s32[32,16]{0,1:T(8,128)}, u32[]{:S(2)}) copy-start(s32[32,16]{0,1:T(8,128)} %param.21) | copy-start | bytes 6148
  45.8 8.3 %copy-start.6 = (s32[32,16]{0,1:T(8,128)S(1)}, s32[32,16]{0,1:T(8,128)}, u32[]{:S(2)}) copy-start(s32[32,16]{0,1:T(8,128)} %param.22) | copy-start | bytes 6148
  45.8 43.4 %copy-start.8 = (f32[512]{0:T(512)S(1)}, f32[512]{0:T(512)}, u32[]{:S(2)}) copy-start(f32[512]{0:T(512)} %param.19) | copy-start | bytes 6148
  92.9 26.0 %copy-start.3 = (bf16[256,512]{1,0:T(8,128)(2,1)S(1)}, bf16[256,512]{1,0:T(8,128)(2,1)}, u32[]{:S(2)}) copy-start(bf16[256,512]{1,0:T(8,128)(2,1)} %param.20) | copy-start | bytes 786436
  95.0 23.9 %all-to-all-start = ((bf16[32,16,512]{2,1,0:T(8,128)(2,1)}), bf16[32,16,512]{2,1,0:T(8,128)(2,1)}, u32[]{:S(2)}, u32[]{:S(2)}) async-start(bf16[32,16,512]{2,1,0:T(8,128)(2,1)} %select_select_fusion), calls=%async_computation.1 | async-start | bytes 1048576 | tf_op jit(solution)/shard_map/all_to_all | solution.py:101
  104.1 44.9 %all-gather.6.cloned.1.call-start = ((), (), s32[]{:S(2)}) async-start(), calls=%async_computation.3 | async-start | bytes 2359296 | tf_op jit(solution)/shard_map/all_gather | solution.py:110
  118.9 32.2 %copy-start.10 = (f32[640]{0:T(1024)S(1)}, f32[640]{0:T(1024)}, u32[]{:S(2)}) copy-start(f32[640]{0:T(1024)} %param.25) | copy-start | bytes 7684
  121.9 0.7 copy-start.2
  122.6 110.3 %all-gather.10.cloned.1.call-start = ((), (), s32[]{:S(2)}) async-start(), calls=%async_computation.5 | async-start | bytes 2162688 | tf_op jit(solution)/shard_map/all_gather | solution.py:135
  122.7 33.4 %copy-start.9 = (f32[64]{0:T(128)}, f32[64]{0:T(128)S(1)}, u32[]{:S(2)}) copy-start(f32[64]{0:T(128)S(1)} %multiply_exponential_fusion) | copy-start | bytes 772
  156.1 2.4 copy-start.4
  156.8 1.6 collective-permute-start
  159.1 156.3 %all-gather.8.cloned.1.call-start = ((), (), s32[]{:S(2)}) async-start(), calls=%async_computation.4 | async-start | bytes 4325376 | tf_op jit(solution)/shard_map/all_gather | solution.py:134
  323.9 3.4 copy-start.1
  338.8 3.4 copy-start.1
  353.9 3.4 copy-start.1
  369.0 3.4 copy-start.1
  384.1 3.4 copy-start.1
  399.2 3.4 copy-start.1
  414.4 3.4 copy-start.1
  429.5 3.4 copy-start.1
Sparse Core Ops, SparseCore 0:
  13.4 28.2 all-gather.11
  54.2 35.0 reduce-scatter.1
  122.7 26.1 all-gather.5
  159.2 73.5 all-gather.9
  235.3 80.0 all-gather.7
where the time goes:
time: 453 us; the launch traced here: 445 us
  waiting for transfers between devices  250 us (55%)
  matrix products  94.6 us (21%)
  other arithmetic  43.6 us (10%)
  local copies, waits for them, and re-layouts  28 us (6%)
  between operations  13.4 us (3%)
  starting transfers between devices  9.84 us (2%)
  loops' own time  5.46 us (1%)
    all_gather x1, waiting for transfers between devices, local(): key_piece = lax.all_gather(key_rows, 'seq', axis=0, tiled=True)  82.5 us
    all_gather x1, waiting for transfers between devices, local(): value_piece = lax.all_gather(value_rows, 'seq', axis=0, tiled=True)  65.2 us
    dot_general x8, matrix products, block_step(): jnp.einsum('qd,kd->qk', query_rows, key_block, preferred_element_type=jnp...  56 us
    reduce_scatter x1, waiting for transfers between devices, local(): lax.psum_scatter(shares.astype(jnp.bfloat16), 'enc', scatter_dimension=1,...  33 us
    all_gather x1, waiting for transfers between devices, local(): lax.all_gather(grouped, 'enc', axis=0, tiled=True)  28.4 us
    reduce_sum x8, other arithmetic, block_step(): new_sum = old_sum * factor + jnp.sum(weights, axis=1)  26.5 us
    all_gather x1, waiting for transfers between devices, local(): full_rows = lax.all_gather(local_tokens, 'enc', axis=1, tiled=True)  26.3 us
    dot_general x8, matrix products, block_step(): jnp.dot(weights.astype(jnp.bfloat16), value_block.astype(jnp.bfloat16), p...  25.4 us
  transfers between devices with their start and end apart: 7, of which 7 were waited for; matrix products, arithmetic and copies ran while one was open for 3% of the time, Pallas kernels for 0%

commit v1 on v0

v1 whole, which is shorter than its diff:
```python
import math

import jax
import jax.numpy as jnp
import numpy as np
from jax import lax
from jax.experimental import pallas as pl
from jax.experimental.pallas import tpu as pltpu
from jax.sharding import PartitionSpec as P

HD = 128
LMAX = 16
NX = 4
EPSILON = 1e-06
THETA = 1000000.0
NEG = -1e30
MESH = pl.DeviceIdType.MESH


def wrap(value, size):
    return lax.rem(value + 2 * size, size)


def remote(src, dst, to, send_sem, recv_sem):
    return pltpu.make_async_remote_copy(
        src_ref=src, dst_ref=dst, send_sem=send_sem, recv_sem=recv_sem, device_id=to, device_id_type=MESH
    )


def sine_cosine(angle):
    turns = jnp.floor(angle * (2.0 / math.pi) + 0.5)
    rest = ((angle - turns * 1.5703125) - turns * 4.837512969970703125e-4) - turns * 7.54978995489188216e-8
    square = rest * rest
    sine = ((-1.9515295891e-4 * square + 8.3321608736e-3) * square - 1.6666654611e-1) * square * rest + rest
    cosine = (
        ((2.443315711809948e-5 * square - 1.388731625493765e-3) * square + 4.166664568298827e-2) * square * square
        - 0.5 * square
        + 1.0
    )
    quadrant = turns - 4.0 * jnp.floor(turns * 0.25)
    odd = (quadrant == 1.0) | (quadrant == 3.0)
    sine, cosine = jnp.where(odd, cosine, sine), jnp.where(odd, sine, cosine)
    sine = jnp.where(quadrant >= 2.0, -sine, sine)
    cosine = jnp.where((quadrant == 1.0) | (quadrant == 2.0), -cosine, cosine)
    return sine, cosine


class EncGather:
    def __init__(self, place, buf, part, sems):
        self.place, self.buf, self.part = place, buf, part
        self.near_send, self.near_recv, self.far_send, self.far_recv, self.give_send, self.give_recv = sems

    def near(self, side, index, h):
        place = self.place
        slot = self.part(self.buf.at[place.ys[index], place.core], h)
        return remote(slot, slot, place.y_side[side], self.near_send.at[side, h], self.near_recv.at[side, h])

    def far(self, side, index):
        place = self.place
        slot = self.part(self.buf.at[place.ys[index], place.core], side)
        return remote(slot, slot, place.y_side[side], self.far_send.at[side], self.far_recv.at[side])

    def give(self, index, h, mine=True):
        place = self.place
        slot = self.part(self.buf.at[place.ys[index], place.core if mine else 1 - place.core], h)
        return remote(slot, slot, place.sibling, self.give_send.at[index, h], self.give_recv.at[index, h])

    def take(self, index):
        for h in range(2):
            self.give(index, h, mine=False).wait_recv()

    def start(self):
        for order in range(2):
            for side in range(2):
                self.near(side, 0, side if order == 0 else 1 - side).start()
        for h in range(2):
            self.give(0, h).start()

    def run(self, work):
        self.take(0)
        work(self.place.ys[0])
        for side in range(2):
            self.near(side, 1 + side, side).wait_recv()
            self.far(side, 1 + side).start()
            self.give(1 + side, side).start()
        for side in range(2):
            self.near(side, 1 + side, 1 - side).wait_recv()
            self.give(1 + side, 1 - side).start()
        for side in range(2):
            self.take(1 + side)
            work(self.place.ys[1 + side])
        for side in range(2):
            self.far(side, 3).wait_recv()
            self.give(3, side).start()
        self.take(3)
        work(self.place.ys[3])

    def drain(self):
        for side in range(2):
            for h in range(2):
                self.near(side, 0, h).wait_send()
            self.far(side, 1 + side).wait_send()
        for index in range(4):
            for h in range(2):
                self.give(index, h).wait_send()


class Place:
    def __init__(self, ny, nz, nx):
        e = lax.axis_index("enc")
        s = lax.axis_index("seq")
        self.e, self.s = e, s
        self.core, self.y = lax.rem(e, 2), lax.div(e, 2)
        self.z, self.x = lax.div(s, nx), lax.rem(s, nx)
        up, down = wrap(self.y + 1, ny), wrap(self.y - 1, ny)
        self.ys = (self.y, down, up, wrap(self.y + 2, ny))
        self.y_side = ((up * 2 + self.core, s), (down * 2 + self.core, s))
        self.sibling = (e + 1 - 2 * self.core, s)
        self.x_side = tuple((e, self.z * nx + wrap(self.x + d, nx)) for d in (1, -1))
        self.z_side = tuple((e, wrap(self.z + d, nz) * nx + self.x) for d in (1, -1))
        self.cols = (self.x, wrap(self.x - 1, nx), wrap(self.x + 1, nx), wrap(self.x + 2, nx))


class PlaneAttention:
    def __init__(self, place, kv, q3, mx, den, acc, sems, nz, nx):
        self.place, self.kv, self.q3, self.mx, self.den, self.acc, self.nz, self.nx = place, kv, q3, mx, den, acc, nz, nx
        self.xs, self.xr, self.hs, self.hr, self.zs, self.zr, self.ss, self.sr = sems
        self.far = nz // 2
        self.half = kv.shape[3]
        self.rows = 2 * self.half
        self.heads = q3.shape[0] // self.rows
        self.group = min(2, self.heads) * self.rows

    def along_x(self, j, side, i):
        place = self.place
        slot = self.kv.at[self.row_at(j), place.core, place.cols[i]]
        return remote(slot, slot, place.x_side[side], self.xs.at[j, side], self.xr.at[j, side])

    def half_on(self, j, side, i):
        place = self.place
        part = pl.ds(side * (self.half // 2), self.half // 2)
        slot = self.kv.at[self.row_at(j), place.core, place.cols[i], part]
        return remote(slot, slot, place.x_side[side], self.hs.at[j, side], self.hr.at[j, side])

    def along_z(self, j, side, i, k):
        place = self.place
        slot = self.kv.at[self.row_at(j), place.core, place.cols[i]]
        at = 4 * (k - 1) + i
        return remote(slot, slot, place.z_side[side], self.zs.at[side, at], self.zr.at[side, at])

    def half_along_z(self, j, side):
        place = self.place
        slot = self.kv.at[self.row_at(j), place.core, place.x, pl.ds(side * (self.half // 2), self.half // 2)]
        at = 4 * (self.far - 1)
        return remote(slot, slot, place.z_side[side], self.zs.at[side, at], self.zr.at[side, at])

    def give(self, j, mine=True):
        place = self.place
        slot = self.kv.at[self.row_at(j), place.core if mine else 1 - place.core]
        return remote(slot, slot, place.sibling, self.ss.at[j], self.sr.at[j])

    def row_at(self, j):
        k = (j + 1) // 2
        return wrap(self.place.z - k, self.nz) if j % 2 == 1 else wrap(self.place.z + k, self.nz)

    def ring_rows(self, k):
        far = self.far
        return [] if not 0 <= k <= far else [0] if k == 0 else [2 * k - 1] if k == far else [2 * k - 1, 2 * k]

    def comes(self, side, k):
        z = self.place.z
        return z >= k if side == 0 else wrap(z + k, self.nz) < self.far

    def goes(self, side, k):
        z = self.place.z
        if side == 0:
            return (z >= k - 1) & (z <= self.nz - 2)
        return wrap(z + k - 1, self.nz) < self.far

    def needed(self, j):
        k = (j + 1) // 2
        z = self.place.z
        return z >= k if j % 2 == 1 else z + k >= self.nz if j else z >= 0

    def start(self):
        for side in range(2):
            self.along_x(0, side, 0).start()

            @pl.when(self.goes(side, 1))
            def _(side=side):
                self.along_z(0, side, 0, 1).start()

    def attend(self, high, low, v, restrict, fresh=False):
        stacked = jnp.concatenate([high, low, high], axis=0)
        pieces = stacked.shape[1] // HD
        parts = [slice(i, i + self.group) for i in range(0, self.heads * self.rows, self.group)]
        scores = [jnp.dot(self.q3[at], stacked, preferred_element_type=jnp.float32) for at in parts]
        for at, score in zip(parts, scores):
            if restrict is not None:
                score = jnp.concatenate([restrict(i, score[:, i * HD : (i + 1) * HD]) for i in range(pieces)], axis=1)
            top = jnp.max(score, axis=1, keepdims=True)
            new = jnp.broadcast_to(top, (self.group, HD)) if fresh else jnp.maximum(self.mx[at], top)
            weights = jnp.exp2(score - jnp.concatenate([new] * pieces, axis=1))
            summed = weights[:, :HD]
            for g in range(1, pieces):
                summed = summed + weights[:, g * HD : (g + 1) * HD]
            product = jnp.dot(weights.astype(jnp.bfloat16), v, preferred_element_type=jnp.float32)
            if fresh:
                self.den[at] = summed
                self.acc[at] = product
            else:
                factor = jnp.exp2(self.mx[at] - new)
                self.den[at] = self.den[at] * factor + summed
                self.acc[at] = self.acc[at] * factor + product
            self.mx[at] = new

    def compute(self, row, c, restrict=None):
        block = self.kv[row, c]
        high = jnp.concatenate([block[i, :, :HD] for i in range(self.nx)], axis=1)
        low = jnp.concatenate([block[i, :, HD : 2 * HD] for i in range(self.nx)], axis=1)
        self.attend(high, low, block[:, :, 2 * HD :].reshape(self.nx * self.half, HD), restrict)

    def own_shard(self, key_high, key_low, value):
        shape = (self.group, HD)
        token = lax.broadcasted_iota(jnp.int32, shape, 0) & (self.rows - 1)
        ahead = lax.broadcasted_iota(jnp.int32, shape, 1) - token
        self.attend(key_high, key_low, value, lambda i, piece: jnp.where(ahead <= -i * HD, piece, NEG), fresh=True)

    def own_row(self, c):
        x = self.place.x

        @pl.when(x > 0)
        def _():
            self.compute(self.place.z, c, lambda i, piece: jnp.where(i < x, piece, NEG))

    def far_rows(self, k, c):
        def step(i, carry):
            row = wrap(self.place.z + k * (2 * i - 1), self.nz)

            @pl.when(row < self.place.z)
            def _():
                self.compute(row, c)

            return carry

        lax.fori_loop(0, len(self.ring_rows(k)), step, 0)

    def pass_rows(self, k, chosen):
        far = self.far
        if not 1 <= k <= far:
            return
        for side in range(2):
            j = min(2 * k - 1 + side, 2 * far - 1)
            mine = [i for i in chosen if k < far or i // 2 == side]
            onward = [i for i in chosen if k + 1 < far or (k + 1 == far and i // 2 == side)]

            @pl.when(self.comes(side, k))
            def _(side=side, j=j, mine=mine):
                for i in mine:
                    self.along_z(j, side, i, k).wait_recv()

            if onward:
                @pl.when(self.goes(side, k + 1))
                def _(side=side, j=j, onward=onward):
                    for i in onward:
                        self.along_z(j, side, i, k + 1).start()

    def early(self, t):
        far = self.far

        @pl.when(self.place.core == 0)
        def _():
            if t == 1:
                for side in range(2):
                    self.along_x(0, side, 1 + side).wait_recv()
                    self.half_on(0, side, 1 + side).start()
                    for direction in range(2):
                        @pl.when(self.goes(direction, 1))
                        def _(side=side, direction=direction):
                            self.along_z(0, direction, 1 + side, 1).start()
            self.pass_rows(t - 2, (0, 1))

        @pl.when(self.place.core == 1)
        def _():
            if 1 <= t <= far:
                for side in range(2):
                    j = min(2 * t - 1 + side, 2 * far - 1)

                    @pl.when(self.comes(side, t))
                    def _(side=side, j=j):
                        if t < far:
                            self.along_z(j, side, 0, t).wait_recv()
                        else:
                            self.half_along_z(j, side).wait_recv()

                    if t < far:
                        @pl.when(self.goes(side, t + 1))
                        def _(side=side, j=j):
                            if t + 1 < far:
                                self.along_z(j, side, 0, t + 1).start()
                            else:
                                self.half_along_z(j, side).start()
                for j in self.ring_rows(t):
                    @pl.when(self.needed(j))
                    def _(j=j):
                        for side in range(2):
                            self.along_x(j, side, 0).start()
            for j in self.ring_rows(t - 1):
                @pl.when(self.needed(j))
                def _(j=j):
                    for side in range(2):
                        self.along_x(j, side, 1 + side).wait_recv()
                        self.half_on(j, side, 1 + side).start()

        for j in self.ring_rows(t - 3):
            @pl.when(self.needed(j))
            def _(j=j):
                self.give(j, mine=False).wait_recv()

    def late(self, t):
        @pl.when(self.place.core == 0)
        def _():
            if t == 2:
                for side in range(2):
                    self.half_on(0, side, 3).wait_recv()
                for direction in range(2):
                    @pl.when(self.goes(direction, 1))
                    def _(direction=direction):
                        self.along_z(0, direction, 3, 1).start()
            self.pass_rows(t - 2, (2, 3))

        for j in self.ring_rows(t - 2):
            @pl.when(self.needed(j))
            def _(j=j):
                @pl.when(self.place.core == 1)
                def _():
                    for side in range(2):
                        self.half_on(j, side, 3).wait_recv()

                self.give(j).start()

    def run(self):
        core, far = self.place.core, self.far
        for t in range(1, far + 4):
            self.early(t)
            if t == 3:
                self.own_row(1 - core)
            elif t > 3:
                self.far_rows(t - 3, 1 - core)
            self.late(t)
            if t == 2:
                self.own_row(core)
            elif 3 <= t <= far + 2:
                self.far_rows(t - 2, core)

    def result(self, h):
        at = slice(h * self.rows, (h + 1) * self.rows)
        return self.acc[at] / jnp.sum(self.den[at], axis=1, keepdims=True)

    def drain(self):
        far = self.far
        for side in range(2):
            self.along_x(0, side, 0).wait_send()
            self.half_on(0, side, 1 + side).wait_send()
        for j in range(2 * far):
            @pl.when(self.needed(j))
            def _(j=j):
                self.give(j).wait_send()

                @pl.when((self.place.core == 1) & (j > 0))
                def _():
                    for side in range(2):
                        self.along_x(j, side, 0).wait_send()
                        self.half_on(j, side, 1 + side).wait_send()

        for side in range(2):
            for k in range(1, far + 1):
                @pl.when(self.goes(side, k))
                def _(side=side, k=k):
                    j = 0 if k == 1 else 2 * k - 3 + side

                    @pl.when(self.place.core == 0)
                    def _():
                        for i in range(4):
                            if k < far or i // 2 == side:
                                self.along_z(j, side, i, k).wait_send()

                    @pl.when(self.place.core == 1)
                    def _():
                        if k < far:
                            self.along_z(j, side, 0, k).wait_send()
                        else:
                            self.half_along_z(j, side).wait_send()


def prefill(
    patches, gain, up_t, up_bias, merge_down, down_bias, text, lengths, offsets, input_gain, qkv_weight, qkv_bias, freq,
    ny, nz, nx,
):
    patch_rows, vision = patches.shape
    units, joined = up_t.shape
    part = patch_rows // 4
    pad = -(-part // 16) * 16
    blocks = 2 * ny
    groups = nz * nx
    slots = groups * LMAX
    rows, width = text.shape
    half = rows // 2
    model = merge_down.shape[1]
    query_width = qkv_weight.shape[1] - HD
    heads = query_width // HD
    far = nz // 2

    def kernel(
        p_ref, g_ref, up_hbm, ub_ref, down_hbm, db_ref, text_ref, len_s, off_s, len_v, off_v, gain_ref, qkv_hbm, qb_ref,
        freq_ref, o_ref,
        buf, turned, up, hid, out, inn, down, w_q, w_kv, kv_bias, sib_out, sib_in, own, rel_out, rel_in, d_out, d_in,
        full, squares, normed, kv, q3, mx, den, acc,
        w_sem, c_send, c_recv, a_send, a_recv, p_send, p_recv, r_send, r_recv, d_send, d_recv,
        fns, fnr, ffs, ffr, fgs, fgr, bns, bnr, bfs, bfr, bgs, bgr,
        xs, xr, hs, hr, zs, zr, ss, sr,
    ):
        place = Place(ny, nz, nx)
        qkv_bias_row = qb_ref[...].reshape(1, query_width + HD)
        input_gain_row = gain_ref[...].reshape(1, model)
        e, s, core, z, x = place.e, place.s, place.core, place.z, place.x

        kv_at = pl.ds(pl.multiple_of(core * HD, HD), HD)
        other_at = pl.ds(pl.multiple_of((1 - core) * HD, HD), HD)
        query_at, rest_at = pl.ds(0, query_width), pl.ds(query_width, HD)
        loads = (
            pltpu.make_async_copy(up_hbm, turned, w_sem.at[0]),
            pltpu.make_async_copy(down_hbm, down, w_sem.at[1]),
            pltpu.make_async_copy(qkv_hbm.at[:, rest_at], w_kv.at[:, kv_at], w_sem.at[2]),
            pltpu.make_async_copy(qkv_hbm.at[:, query_at], w_q, w_sem.at[3]),
        )
        for load in loads:
            load.start()
        barrier = pltpu.get_barrier_semaphore()

        def greet(p, carry):
            pl.semaphore_signal(barrier, inc=1, device_id=(e, wrap(s + p, groups)), device_id_type=MESH)
            return carry

        lax.fori_loop(1, groups, greet, 0)
        for other in (*place.y_side, place.sibling):
            pl.semaphore_signal(barrier, inc=1, device_id=other, device_id_type=MESH)

        front = EncGather(place, buf, lambda block, h: block.at[pl.ds(2 * h, 2)], (fns, fnr, ffs, ffr, fgs, fgr))
        values = p_ref[...].astype(jnp.float32)
        mean_square = jnp.mean(values * values, axis=1, keepdims=True)
        vision_rows = (values * lax.rsqrt(mean_square + EPSILON) * g_ref[...].reshape(1, vision)).astype(jnp.bfloat16)
        to = lax.broadcasted_iota(jnp.int32, (4 * pad, patch_rows), 0)
        source = lax.broadcasted_iota(jnp.int32, (4 * pad, patch_rows), 1)
        moved = (source == 4 * (to % pad) + to // pad) & (to % pad < part)
        order = jnp.where(moved, 1.0, 0.0).astype(jnp.bfloat16)
        sorted_rows = jnp.dot(order, vision_rows, preferred_element_type=jnp.float32).astype(jnp.bfloat16)
        for q in range(4):
            buf[place.y, core, q] = sorted_rows[q * pad : (q + 1) * pad]
        pl.semaphore_wait(barrier, groups - 1 + 3)
        front.start()
        kv_columns = remote(
            qkv_hbm.at[:, rest_at], w_kv.at[:, kv_at], place.sibling, c_send.at[0], c_recv.at[0]
        )
        kv_columns.start()
        kv_bias[core] = qkv_bias_row[:, query_width:]
        bias_columns = remote(kv_bias.at[core], kv_bias.at[core], place.sibling, c_send.at[1], c_recv.at[1])
        bias_columns.start()

        loads[0].wait()
        if joined % 512 == 0:
            def turn(i, carry):
                at = pl.ds(pl.multiple_of(i * 512, 512), 512)
                up[at, :] = turned[:, at].T
                return carry

            lax.fori_loop(0, joined // 512, turn, 0)
        else:
            up[...] = turned[...].T

        lane = lax.broadcasted_iota(jnp.int32, (1, blocks * pad), 1)
        merged = jnp.where(lane % pad < part, lane // pad * part + lane % pad, -1)
        code = jnp.full((1, blocks * pad), -1, jnp.int32)
        begin = jnp.int32(0)
        for j in range(len_s.shape[0]):
            end = begin + len_s[j, s]
            inside = (merged >= begin) & (merged < end)
            code = jnp.where(inside, off_s[j, s] // rows * LMAX + merged - begin, code)
            begin = end
        slot = lax.broadcasted_iota(jnp.int32, (slots, blocks * pad), 0)
        pick = jnp.where(slot == code, 1.0, 0.0).astype(jnp.bfloat16)

        ours = off_v[...] // rows == s
        first = jnp.sum(jnp.where(ours, off_v[...] - s * rows, 0).astype(jnp.float32), axis=0, keepdims=True)
        count = jnp.sum(jnp.where(ours, len_v[...], 0).astype(jnp.float32), axis=0, keepdims=True)
        group = lax.broadcasted_iota(jnp.int32, (groups, slots), 0)
        position = lax.broadcasted_iota(jnp.int32, (groups, slots), 1)
        spread_groups = jnp.where(position // LMAX == group, 1.0, 0.0).astype(jnp.bfloat16)
        both = jnp.concatenate([jnp.broadcast_to(first, (8, groups)), jnp.broadcast_to(count, (8, groups))], axis=0)
        both = jnp.dot(both.astype(jnp.bfloat16), spread_groups, preferred_element_type=jnp.float32)
        index = (lax.broadcasted_iota(jnp.int32, (1, slots), 1) % LMAX).astype(jnp.float32)
        target = jnp.where(index < both[8:9], both[:1] + index, -1.0)
        token = lax.broadcasted_iota(jnp.int32, (rows, slots), 0).astype(jnp.float32)
        placing = jnp.where(token == target, 1.0, 0.0)
        covered = jnp.sum(placing, axis=1, keepdims=True) > 0.5

        def merge(y):
            grouped = jnp.concatenate([buf[y, :, q].reshape(2 * pad, vision) for q in range(4)], axis=1)
            inner = jnp.dot(grouped, up[...], preferred_element_type=jnp.float32) + ub_ref[...].reshape(1, units)
            inner = 0.5 * inner * (1.0 + lax.erf(inner * math.sqrt(0.5)))
            hid[y] = inner.astype(jnp.bfloat16)

        front.run(merge)

        chosen = jnp.dot(pick, hid[...].reshape(blocks * pad, units), preferred_element_type=jnp.float32)
        out[...] = chosen.astype(jnp.bfloat16).reshape(groups, LMAX, units)

        def swap(p, at, arrives):
            return remote(out.at[at], inn.at[arrives], (e, at), a_send.at[p], a_recv.at[p])

        def begin_swap(p, carry):
            swap(p, wrap(s + p, groups), s).start()
            return carry

        lax.fori_loop(1, groups, begin_swap, 0)
        inn[s] = out[s]
        loads[1].wait()

        def end_swap(p, carry):
            swap(p, wrap(s + p, groups), wrap(s - p + groups, groups)).wait()
            return carry

        lax.fori_loop(1, groups, end_swap, 0)
        placed = jnp.dot(
            placing.astype(jnp.bfloat16), inn[...].reshape(slots, units), preferred_element_type=jnp.float32
        ).astype(jnp.bfloat16)

        targets = (place.ys[3], place.ys[2], place.ys[1], place.y)

        def share(y_to, c_to):
            start = pl.multiple_of((y_to * 2 + c_to) * width, width)
            return jnp.dot(placed, down[:, pl.ds(start, width)], preferred_element_type=jnp.float32)

        def pair(i):
            return remote(sib_out.at[i], sib_in.at[i], place.sibling, p_send.at[i], p_recv.at[i])

        def relay(side):
            return remote(rel_out.at[side], rel_in.at[side], place.y_side[side], r_send.at[side], r_recv.at[side])

        def deliver(side, h):
            return remote(
                d_out.at[side, h], d_in.at[side, h], place.y_side[side], d_send.at[side, h], d_recv.at[side, h]
            )

        halves = (slice(0, half), slice(half, rows))
        for i in range(4):
            sib_out[i] = share(targets[i], 1 - core).astype(jnp.bfloat16)
            pair(i).start()
        for i in range(4):
            own[i] = share(targets[i], core)
        pair(0).wait_recv()
        for side in range(2):
            at = halves[side]
            rel_out[side] = (own[0, at] + sib_in[0, at].astype(jnp.float32)).astype(jnp.bfloat16)
            relay(side).start()
        for side in range(2):
            pair(1 + side).wait_recv()
            own[1 + side] = own[1 + side] + sib_in[1 + side].astype(jnp.float32)
            d_out[side, 1 - side] = own[1 + side, halves[1 - side]].astype(jnp.bfloat16)
            deliver(side, 1 - side).start()
        pair(3).wait_recv()
        own[3] = own[3] + sib_in[3].astype(jnp.float32) + db_ref[...].reshape(1, width)
        for side in range(2):
            relay(side).wait_recv()
            d_out[side, side] = (own[1 + side, halves[side]] + rel_in[side].astype(jnp.float32)).astype(jnp.bfloat16)
            deliver(side, side).start()

        token_id = lax.broadcasted_iota(jnp.int32, (rows, HD), 0) + s * rows
        sine, cosine = sine_cosine(token_id.astype(jnp.float32) * freq_ref[...])
        signed = jnp.where(lax.broadcasted_iota(jnp.int32, (rows, HD), 1) < HD // 2, -sine, sine)

        def rotate(block):
            return block * cosine + pltpu.roll(block, HD // 2, 1) * signed

        back = EncGather(place, full, lambda block, h: block.at[pl.ds(h * half, half)], (bns, bnr, bfs, bfr, bgs, bgr))
        for h in range(2):
            at = halves[h]
            total = own[3, at]
            for side in range(2):
                deliver(side, h).wait_recv()
                total = total + d_in[side, h].astype(jnp.float32)
            kept = jnp.where(covered[at], total, text_ref[at].astype(jnp.float32))
            full[place.y, core, at] = kept.astype(jnp.bfloat16)
        back.start()
        squares[...] = jnp.zeros(squares.shape, jnp.float32)

        def add_squares(y):
            for c in range(2):
                block = full[y, c].astype(jnp.float32)
                block = block * block
                for g in range(width // HD):
                    squares[...] += block[:, g * HD : (g + 1) * HD]

        back.run(add_squares)

        scale = lax.rsqrt(jnp.sum(squares[...], axis=1, keepdims=True) * (1.0 / model) + EPSILON)
        for block in range(blocks):
            at = slice(block * width, (block + 1) * width)
            normed[:, at] = (full[block // 2, block % 2].astype(jnp.float32) * scale * input_gain_row[:, at]).astype(
                jnp.bfloat16
            )
        loads[2].wait()
        remote(
            qkv_hbm.at[:, rest_at], w_kv.at[:, other_at], place.sibling, c_send.at[0], c_recv.at[0]
        ).wait_recv()
        remote(kv_bias.at[core], kv_bias.at[1 - core], place.sibling, c_send.at[1], c_recv.at[1]).wait_recv()
        both = jnp.dot(normed[...], w_kv[...], preferred_element_type=jnp.float32)
        key = rotate(both[:, :HD] + kv_bias[0]).T
        key_high = key.astype(jnp.bfloat16)
        key_low = (key - key_high.astype(jnp.float32)).astype(jnp.bfloat16)
        value = (both[:, HD:] + kv_bias[1]).astype(jnp.bfloat16)

        for c in range(2):
            @pl.when(core == c)
            def _(c=c):
                kv[z, c, x, :, :HD] = key_high[:, halves[c]]
                kv[z, c, x, :, HD : 2 * HD] = key_low[:, halves[c]]
                kv[z, c, x, :, 2 * HD :] = value[halves[c]]

        plane = PlaneAttention(place, kv, q3, mx, den, acc, (xs, xr, hs, hr, zs, zr, ss, sr), nz, nx)
        plane.start()

        loads[3].wait()
        scaling = HD ** (-0.5) * math.log2(math.e)
        for pair_of in range(heads // 2):
            at = slice(pair_of * 2 * HD, (pair_of + 1) * 2 * HD)
            query = jnp.dot(normed[...], w_q[:, at], preferred_element_type=jnp.float32) + qkv_bias_row[:, at]
            for i in range(2):
                rows_of = slice((pair_of * 2 + i) * rows, (pair_of * 2 + i + 1) * rows)
                turned_query = rotate(query[:, i * HD : (i + 1) * HD]) * scaling
                high = turned_query.astype(jnp.bfloat16)
                q3[rows_of, :HD] = high
                q3[rows_of, HD : 2 * HD] = high
                q3[rows_of, 2 * HD :] = (turned_query - high.astype(jnp.float32)).astype(jnp.bfloat16)

        plane.own_shard(key_high, key_low, value)
        plane.run()
        for h in range(heads):
            o_ref[:, h * HD : (h + 1) * HD] = plane.result(h).astype(o_ref.dtype)

        front.drain()
        back.drain()
        kv_columns.wait_send()
        bias_columns.wait_send()
        for i in range(4):
            pair(i).wait_send()
        for side in range(2):
            relay(side).wait_send()
            for h in range(2):
                deliver(side, h).wait_send()
        plane.drain()

    dma = pltpu.SemaphoreType.DMA
    bf16, f32 = jnp.bfloat16, jnp.float32
    vmem = pl.BlockSpec(memory_space=pltpu.VMEM)
    smem = pl.BlockSpec(memory_space=pltpu.SMEM)
    any_space = pl.BlockSpec(memory_space=pl.ANY)
    enc_sems = [dma((2, 2)), dma((2, 2)), dma((2,)), dma((2,)), dma((4, 2)), dma((4, 2))]
    return pl.pallas_call(
        kernel,
        out_shape=jax.ShapeDtypeStruct((rows, query_width), bf16),
        in_specs=[
            vmem, vmem, any_space, vmem, any_space, vmem, vmem, smem, smem, vmem, vmem, vmem, any_space, vmem, vmem,
        ],
        out_specs=vmem,
        scratch_shapes=[
            pltpu.VMEM((ny, 2, 4, pad, vision), bf16),
            pltpu.VMEM((units, joined), bf16),
            pltpu.VMEM((joined, units), bf16),
            pltpu.VMEM((ny, 2 * pad, units), bf16),
            pltpu.VMEM((groups, LMAX, units), bf16),
            pltpu.VMEM((groups, LMAX, units), bf16),
            pltpu.VMEM(merge_down.shape, bf16),
            pltpu.VMEM((model, query_width), bf16),
            pltpu.VMEM((model, 2 * HD), bf16),
            pltpu.VMEM((2, 1, HD), f32),
            pltpu.VMEM((4, rows, width), bf16),
            pltpu.VMEM((4, rows, width), bf16),
            pltpu.VMEM((4, rows, width), f32),
            pltpu.VMEM((2, half, width), bf16),
            pltpu.VMEM((2, half, width), bf16),
            pltpu.VMEM((2, 2, half, width), bf16),
            pltpu.VMEM((2, 2, half, width), bf16),
            pltpu.VMEM((ny, 2, rows, width), bf16),
            pltpu.VMEM((rows, HD), f32),
            pltpu.VMEM((rows, model), bf16),
            pltpu.VMEM((nz, 2, nx, half, 3 * HD), bf16),
            pltpu.VMEM((heads * rows, 3 * HD), bf16),
            pltpu.VMEM((heads * rows, HD), f32),
            pltpu.VMEM((heads * rows, HD), f32),
            pltpu.VMEM((heads * rows, HD), f32),
            dma((4,)),
            dma((2,)),
            dma((2,)),
            dma((groups,)),
            dma((groups,)),
            dma((4,)),
            dma((4,)),
            dma((2,)),
            dma((2,)),
            dma((2, 2)),
            dma((2, 2)),
            *enc_sems,
            *enc_sems,
            dma((nz, 2)),
            dma((nz, 2)),
            dma((nz, 2)),
            dma((nz, 2)),
            dma((2, 4 * far)),
            dma((2, 4 * far)),
            dma((nz,)),
            dma((nz,)),
        ],
        compiler_params=pltpu.CompilerParams(
            collective_id=1, has_side_effects=True, vmem_limit_bytes=56 * 1024 * 1024
        ),
        name="prefill",
    )(
        patches, gain, up_t, up_bias, merge_down, down_bias, text, lengths, offsets, lengths, offsets, input_gain,
        qkv_weight, qkv_bias, freq,
    )


def local(
    patches, vision_gain, merge_up, merge_up_bias, merge_down, merge_down_bias, text_embed, image_lengths, image_offsets,
    input_gain, qkv_weight, qkv_bias,
):
    freq = np.exp(np.arange(HD // 2) * (-2.0 * np.log(THETA) / HD)).astype(np.float32)
    return prefill(
        patches[0], vision_gain, merge_up.T, merge_up_bias, merge_down, merge_down_bias, text_embed,
        image_lengths.T, image_offsets.T, input_gain, qkv_weight, qkv_bias,
        jnp.asarray(np.concatenate([freq, freq])[None]),
        lax.axis_size("enc") // 2, lax.axis_size("seq") // NX, NX,
    )


def solution(mesh):
    in_specs = (
        P("seq", "enc", None),
        P(),
        P(None, "enc"),
        P("enc"),
        P("enc", None),
        P("enc"),
        P("seq", "enc"),
        P(),
        P(),
        P(),
        P(None, "enc"),
        P("enc"),
    )
    out_specs = P("seq", "enc")
    return jax.shard_map(local, mesh=mesh, in_specs=in_specs, out_specs=out_specs, check_vma=False)
```

time: 453 us -> 99.3 us (0.22)
  the two profiles are of different devices: /device:TPU:249 before, /device:TPU:193 now
where the time goes in v1:
time: 99.3 us; the launch traced here: 99.2 us
  Pallas kernels  97.5 us (98%)
  local copies, waits for them, and re-layouts  1.67 us (2%)
    pallas_call x1, Pallas kernels, prefill(): pl.pallas_call(kernel, out_shape=jax.ShapeDtypeStruct((rows, query_width)...  97.5 us

profile of v1, /device:TPU:193, one launch (start us, length us, event | category | flops | bytes accessed | tf_op | source)
XLA Modules:
  0.0 99.2 jit_solution(9976679175349124048)
XLA Ops:
  0.0 97.5 %prefill.1 = bf16[256,512]{1,0:T(8,128)(2,1)} custom-call(bf16[112,1280]{1,0:T(8,128)(2,1)} %bitcast.5, f32[1280]{0:T(1024)} %g_ref.1, bf16[320,5120]{1,0:T(8,128)(2,1)} %bitcast.4, f32[320]{0:T(512)} %ub_ref.1, bf16[320,4096]{1,0:T(8,128)(2,1)} %down_hbm.1, f32[512]{0:T(512)} %db_ref.1, bf16[256,512]{1,0:T(8,128)(2,1)} %text_ref.1, s32[16,32]{1,0:T(8,128)} %bitcast.6, ...), custom_call_target="tpu_custom_call" | custom-call | tf_op jit(solution)/shard_map/prefill/pallas_call | solution.py:669
  97.5 1.7 %copy.15 = bf16[256,512]{1,0:T(8,128)(2,1)} copy(bf16[256,512]{1,0:T(8,128)(2,1)} %prefill.1) | data formatting | bytes 524288

commit v2 on v1

--- a/solution.py
+++ b/solution.py
@@ -69,31 +69,26 @@
         for h in range(2):
             self.give(index, h, mine=False).wait_recv()
 
-    def start(self):
-        for order in range(2):
-            for side in range(2):
-                self.near(side, 0, side if order == 0 else 1 - side).start()
-        for h in range(2):
-            self.give(0, h).start()
-
-    def run(self, work):
-        self.take(0)
-        work(self.place.ys[0])
+    def start(self, h):
+        for side in range(2):
+            self.near(side, 0, h).start()
+        self.give(0, h).start()
+
+    def relay(self):
         for side in range(2):
             self.near(side, 1 + side, side).wait_recv()
             self.far(side, 1 + side).start()
             self.give(1 + side, side).start()
+
+    def finish_near(self):
         for side in range(2):
             self.near(side, 1 + side, 1 - side).wait_recv()
             self.give(1 + side, 1 - side).start()
-        for side in range(2):
-            self.take(1 + side)
-            work(self.place.ys[1 + side])
+
+    def finish_far(self):
         for side in range(2):
             self.far(side, 3).wait_recv()
             self.give(3, side).start()
-        self.take(3)
-        work(self.place.ys[3])
 
     def drain(self):
         for side in range(2):
@@ -312,7 +307,8 @@
                         self.along_x(j, side, 1 + side).wait_recv()
                         self.half_on(j, side, 1 + side).start()
 
-        for j in self.ring_rows(t - 3):
+    def from_sibling(self, k):
+        for j in self.ring_rows(k):
             @pl.when(self.needed(j))
             def _(j=j):
                 self.give(j, mine=False).wait_recv()
@@ -343,11 +339,13 @@
         core, far = self.place.core, self.far
         for t in range(1, far + 4):
             self.early(t)
-            if t == 3:
-                self.own_row(1 - core)
-            elif t > 3:
+            if t > 3:
+                self.from_sibling(t - 3)
                 self.far_rows(t - 3, 1 - core)
             self.late(t)
+            if t == 3:
+                self.from_sibling(0)
+                self.own_row(1 - core)
             if t == 2:
                 self.own_row(core)
             elif 3 <= t <= far + 2:
@@ -458,7 +456,8 @@
         for q in range(4):
             buf[place.y, core, q] = sorted_rows[q * pad : (q + 1) * pad]
         pl.semaphore_wait(barrier, groups - 1 + 3)
-        front.start()
+        front.start(0)
+        front.start(1)
         kv_columns = remote(
             qkv_hbm.at[:, rest_at], w_kv.at[:, kv_at], place.sibling, c_send.at[0], c_recv.at[0]
         )
@@ -468,15 +467,16 @@
         bias_columns.start()
 
         loads[0].wait()
-        if joined % 512 == 0:
-            def turn(i, carry):
-                at = pl.ds(pl.multiple_of(i * 512, 512), 512)
-                up[at, :] = turned[:, at].T
-                return carry
-
-            lax.fori_loop(0, joined // 512, turn, 0)
-        else:
-            up[...] = turned[...].T
+        def turn(i, carry):
+            at = pl.ds(pl.multiple_of(i * 512, 512), 512)
+            up[at, :] = turned[:, at].T
+            return carry
+
+        turns = joined // 512
+        lax.fori_loop(0, turns // 2, turn, 0)
+        front.relay()
+        lax.fori_loop(turns // 2, turns, turn, 0)
+        front.finish_near()
 
         lane = lax.broadcasted_iota(jnp.int32, (1, blocks * pad), 1)
         merged = jnp.where(lane % pad < part, lane // pad * part + lane % pad, -1)
@@ -504,13 +504,27 @@
         placing = jnp.where(token == target, 1.0, 0.0)
         covered = jnp.sum(placing, axis=1, keepdims=True) > 0.5
 
-        def merge(y):
-            grouped = jnp.concatenate([buf[y, :, q].reshape(2 * pad, vision) for q in range(4)], axis=1)
+        def merge(*chips):
+            grouped = jnp.concatenate(
+                [
+                    jnp.concatenate([buf[y, :, q].reshape(2 * pad, vision) for q in range(4)], axis=1)
+                    for y in chips
+                ],
+                axis=0,
+            )
             inner = jnp.dot(grouped, up[...], preferred_element_type=jnp.float32) + ub_ref[...].reshape(1, units)
-            inner = 0.5 * inner * (1.0 + lax.erf(inner * math.sqrt(0.5)))
-            hid[y] = inner.astype(jnp.bfloat16)
-
-        front.run(merge)
+            inner = (0.5 * inner * (1.0 + lax.erf(inner * math.sqrt(0.5)))).astype(jnp.bfloat16)
+            for i, y in enumerate(chips):
+                hid[y] = inner[i * 2 * pad : (i + 1) * 2 * pad]
+
+        front.take(0)
+        merge(place.ys[0])
+        front.take(1)
+        front.take(2)
+        merge(place.ys[1], place.ys[2])
+        front.finish_far()
+        front.take(3)
+        merge(place.ys[3])
 
         chosen = jnp.dot(pick, hid[...].reshape(blocks * pad, units), preferred_element_type=jnp.float32)
         out[...] = chosen.astype(jnp.bfloat16).reshape(groups, LMAX, units)
@@ -527,7 +541,7 @@
         loads[1].wait()
 
         def end_swap(p, carry):
-            swap(p, wrap(s + p, groups), wrap(s - p + groups, groups)).wait()
+            swap(p, wrap(s + p, groups), wrap(s - p + groups, groups)).wait_recv()
             return carry
 
         lax.fori_loop(1, groups, end_swap, 0)
@@ -591,7 +605,7 @@
                 total = total + d_in[side, h].astype(jnp.float32)
             kept = jnp.where(covered[at], total, text_ref[at].astype(jnp.float32))
             full[place.y, core, at] = kept.astype(jnp.bfloat16)
-        back.start()
+            back.start(h)
         squares[...] = jnp.zeros(squares.shape, jnp.float32)
 
         def add_squares(y):
@@ -601,7 +615,16 @@
                 for g in range(width // HD):
                     squares[...] += block[:, g * HD : (g + 1) * HD]
 
-        back.run(add_squares)
+        back.take(0)
+        add_squares(place.ys[0])
+        back.relay()
+        back.finish_near()
+        for i in range(1, 3):
+            back.take(i)
+            add_squares(place.ys[i])
+        back.finish_far()
+        back.take(3)
+        add_squares(place.ys[3])
 
         scale = lax.rsqrt(jnp.sum(squares[...], axis=1, keepdims=True) * (1.0 / model) + EPSILON)
         for block in range(blocks):
@@ -648,6 +671,11 @@
         for h in range(heads):
             o_ref[:, h * HD : (h + 1) * HD] = plane.result(h).astype(o_ref.dtype)
 
+        def sent_swap(p, carry):
+            swap(p, wrap(s + p, groups), s).wait_send()
+            return carry
+
+        lax.fori_loop(1, groups, sent_swap, 0)
         front.drain()
         back.drain()
         kv_columns.wait_send()

time: 99.3 us -> 98.8 us (level)
  the two profiles are of different devices: /device:TPU:193 before, /device:TPU:249 now
where the time goes in v2:
time: 98.8 us; the launch traced here: 98.1 us
  Pallas kernels  96.4 us (98%)
  local copies, waits for them, and re-layouts  1.67 us (2%)
    pallas_call x1, Pallas kernels, prefill(): pl.pallas_call(kernel, out_shape=jax.ShapeDtypeStruct((rows, query_width)...  96.4 us

profile of v2, /device:TPU:249, one launch (start us, length us, event | category | flops | bytes accessed | tf_op | source)
XLA Modules:
  0.0 98.1 jit_solution(9684014807030409965)
XLA Ops:
  0.0 96.4 %prefill.1 = bf16[256,512]{1,0:T(8,128)(2,1)} custom-call(bf16[112,1280]{1,0:T(8,128)(2,1)} %bitcast.5, f32[1280]{0:T(1024)} %g_ref.1, bf16[320,5120]{1,0:T(8,128)(2,1)} %bitcast.4, f32[320]{0:T(512)} %ub_ref.1, bf16[320,4096]{1,0:T(8,128)(2,1)} %down_hbm.1, f32[512]{0:T(512)} %db_ref.1, bf16[256,512]{1,0:T(8,128)(2,1)} %text_ref.1, s32[16,32]{1,0:T(8,128)} %bitcast.6, ...), custom_call_target="tpu_custom_call" | custom-call | tf_op jit(solution)/shard_map/prefill/pallas_call | solution.py:697
  96.4 1.7 %copy.15 = bf16[256,512]{1,0:T(8,128)(2,1)} copy(bf16[256,512]{1,0:T(8,128)(2,1)} %prefill.1) | data formatting | bytes 524288

commit v3 on v2

--- a/solution.py
+++ b/solution.py
@@ -46,23 +46,23 @@
 
 
 class EncGather:
-    def __init__(self, place, buf, part, sems):
-        self.place, self.buf, self.part = place, buf, part
+    def __init__(self, place, half, sems, shared):
+        self.place, self.half, self.shared = place, half, shared
         self.near_send, self.near_recv, self.far_send, self.far_recv, self.give_send, self.give_recv = sems
 
     def near(self, side, index, h):
         place = self.place
-        slot = self.part(self.buf.at[place.ys[index], place.core], h)
+        slot = self.half(place.ys[index], place.core, h)
         return remote(slot, slot, place.y_side[side], self.near_send.at[side, h], self.near_recv.at[side, h])
 
     def far(self, side, index):
         place = self.place
-        slot = self.part(self.buf.at[place.ys[index], place.core], side)
+        slot = self.half(place.ys[index], place.core, side)
         return remote(slot, slot, place.y_side[side], self.far_send.at[side], self.far_recv.at[side])
 
     def give(self, index, h, mine=True):
         place = self.place
-        slot = self.part(self.buf.at[place.ys[index], place.core if mine else 1 - place.core], h)
+        slot = self.half(place.ys[index], place.core if mine else 1 - place.core, h)
         return remote(slot, slot, place.sibling, self.give_send.at[index, h], self.give_recv.at[index, h])
 
     def take(self, index):
@@ -72,30 +72,34 @@
     def start(self, h):
         for side in range(2):
             self.near(side, 0, h).start()
-        self.give(0, h).start()
+        self.share(0, h)
+
+    def share(self, index, h):
+        if self.shared:
+            self.give(index, h).start()
 
     def relay(self):
         for side in range(2):
             self.near(side, 1 + side, side).wait_recv()
             self.far(side, 1 + side).start()
-            self.give(1 + side, side).start()
+            self.share(1 + side, side)
 
     def finish_near(self):
         for side in range(2):
             self.near(side, 1 + side, 1 - side).wait_recv()
-            self.give(1 + side, 1 - side).start()
+            self.share(1 + side, 1 - side)
 
     def finish_far(self):
         for side in range(2):
             self.far(side, 3).wait_recv()
-            self.give(3, side).start()
+            self.share(3, side)
 
     def drain(self):
         for side in range(2):
             for h in range(2):
                 self.near(side, 0, h).wait_send()
             self.far(side, 1 + side).wait_send()
-        for index in range(4):
+        for index in range(4 if self.shared else 0):
             for h in range(2):
                 self.give(index, h).wait_send()
 
@@ -123,8 +127,9 @@
         self.far = nz // 2
         self.half = kv.shape[3]
         self.rows = 2 * self.half
-        self.heads = q3.shape[0] // self.rows
-        self.group = min(2, self.heads) * self.rows
+        self.heads = q3.shape[0]
+        self.together = min(2, self.heads)
+        self.group = self.together * self.rows
 
     def along_x(self, j, side, i):
         place = self.place
@@ -189,7 +194,10 @@
         stacked = jnp.concatenate([high, low, high], axis=0)
         pieces = stacked.shape[1] // HD
         parts = [slice(i, i + self.group) for i in range(0, self.heads * self.rows, self.group)]
-        scores = [jnp.dot(self.q3[at], stacked, preferred_element_type=jnp.float32) for at in parts]
+        queries = [
+            self.q3[h : h + self.together].reshape(self.group, 3 * HD) for h in range(0, self.heads, self.together)
+        ]
+        scores = [jnp.dot(query, stacked, preferred_element_type=jnp.float32) for query in queries]
         for at, score in zip(parts, scores):
             if restrict is not None:
                 score = jnp.concatenate([restrict(i, score[:, i * HD : (i + 1) * HD]) for i in range(pieces)], axis=1)
@@ -209,24 +217,23 @@
                 self.acc[at] = self.acc[at] * factor + product
             self.mx[at] = new
 
-    def compute(self, row, c, restrict=None):
+    def compute(self, row, c, restrict=None, fresh=False):
         block = self.kv[row, c]
         high = jnp.concatenate([block[i, :, :HD] for i in range(self.nx)], axis=1)
         low = jnp.concatenate([block[i, :, HD : 2 * HD] for i in range(self.nx)], axis=1)
-        self.attend(high, low, block[:, :, 2 * HD :].reshape(self.nx * self.half, HD), restrict)
-
-    def own_shard(self, key_high, key_low, value):
+        self.attend(high, low, block[:, :, 2 * HD :].reshape(self.nx * self.half, HD), restrict, fresh)
+
+    def own_row(self, c, fresh):
+        x = self.place.x
         shape = (self.group, HD)
         token = lax.broadcasted_iota(jnp.int32, shape, 0) & (self.rows - 1)
         ahead = lax.broadcasted_iota(jnp.int32, shape, 1) - token
-        self.attend(key_high, key_low, value, lambda i, piece: jnp.where(ahead <= -i * HD, piece, NEG), fresh=True)
-
-    def own_row(self, c):
-        x = self.place.x
-
-        @pl.when(x > 0)
-        def _():
-            self.compute(self.place.z, c, lambda i, piece: jnp.where(i < x, piece, NEG))
+
+        def restrict(i, piece):
+            limit = jnp.where(x > i, 2 * self.rows, jnp.where(x == i, 0, -2 * self.rows)) - c * self.half
+            return jnp.where(ahead <= limit, piece, NEG)
+
+        self.compute(self.place.z, c, restrict, fresh)
 
     def far_rows(self, k, c):
         def step(i, carry):
@@ -335,7 +342,7 @@
 
                 self.give(j).start()
 
-    def run(self):
+    def run(self, queries_here):
         core, far = self.place.core, self.far
         for t in range(1, far + 4):
             self.early(t)
@@ -345,9 +352,10 @@
             self.late(t)
             if t == 3:
                 self.from_sibling(0)
-                self.own_row(1 - core)
+                self.own_row(1 - core, False)
             if t == 2:
-                self.own_row(core)
+                queries_here()
+                self.own_row(core, True)
             elif 3 <= t <= far + 2:
                 self.far_rows(t - 2, core)
 
@@ -400,6 +408,7 @@
     part = patch_rows // 4
     pad = -(-part // 16) * 16
     blocks = 2 * ny
+    wide = 2 * text.shape[1]
     groups = nz * nx
     slots = groups * LMAX
     rows, width = text.shape
@@ -412,28 +421,48 @@
     def kernel(
         p_ref, g_ref, up_hbm, ub_ref, down_hbm, db_ref, text_ref, len_s, off_s, len_v, off_v, gain_ref, qkv_hbm, qb_ref,
         freq_ref, o_ref,
-        buf, turned, up, hid, out, inn, down, w_q, w_kv, kv_bias, sib_out, sib_in, own, rel_out, rel_in, d_out, d_in,
-        full, squares, normed, kv, q3, mx, den, acc,
-        w_sem, c_send, c_recv, a_send, a_recv, p_send, p_recv, r_send, r_recv, d_send, d_recv,
-        fns, fnr, ffs, ffr, fgs, fgr, bns, bnr, bfs, bfr, bgs, bgr,
+        buf, turned, up, hid, out, inn, down, w_q, w_kv, qkv_bias_of, down_bias_of, text_of, placed_out, placed_in,
+        own, rel_out, rel_in, d_out, d_in, full, squares, normed, kv, q3, q_out, mx, den, acc,
+        w_sem, c_send, c_recv, a_send, a_recv, r_send, r_recv, d_send, d_recv,
+        fns, fnr, ffs, ffr, fgs, fgr, bns, bnr, bfs, bfr,
         xs, xr, hs, hr, zs, zr, ss, sr,
     ):
         place = Place(ny, nz, nx)
-        qkv_bias_row = qb_ref[...].reshape(1, query_width + HD)
-        input_gain_row = gain_ref[...].reshape(1, model)
         e, s, core, z, x = place.e, place.s, place.core, place.z, place.x
-
-        kv_at = pl.ds(pl.multiple_of(core * HD, HD), HD)
-        other_at = pl.ds(pl.multiple_of((1 - core) * HD, HD), HD)
+        other = 1 - core
+
         query_at, rest_at = pl.ds(0, query_width), pl.ds(query_width, HD)
+
+        def lanes(c, size):
+            return pl.ds(pl.multiple_of(c * size, size), size)
+
+        def tokens(c):
+            return pl.ds(pl.multiple_of(c * half, half), half)
+
         loads = (
             pltpu.make_async_copy(up_hbm, turned, w_sem.at[0]),
-            pltpu.make_async_copy(down_hbm, down, w_sem.at[1]),
-            pltpu.make_async_copy(qkv_hbm.at[:, rest_at], w_kv.at[:, kv_at], w_sem.at[2]),
-            pltpu.make_async_copy(qkv_hbm.at[:, query_at], w_q, w_sem.at[3]),
+            pltpu.make_async_copy(down_hbm, down.at[core], w_sem.at[1]),
+            pltpu.make_async_copy(qkv_hbm.at[:, rest_at], w_kv.at[:, lanes(core, HD)], w_sem.at[2]),
+            pltpu.make_async_copy(qkv_hbm.at[:, query_at], w_q.at[core], w_sem.at[3]),
         )
         for load in loads:
             load.start()
+
+        def to_sibling(i, src, dst):
+            return remote(src, dst, place.sibling, c_send.at[i], c_recv.at[i])
+
+        def gift(i, c):
+            return (
+                lambda: to_sibling(0, qkv_bias_of.at[core], qkv_bias_of.at[c]),
+                lambda: to_sibling(1, down_bias_of.at[core], down_bias_of.at[c]),
+                lambda: to_sibling(2, text_ref.at[tokens(other)], text_of.at[:, lanes(c, width)]),
+                lambda: to_sibling(3, qkv_hbm.at[:, rest_at], w_kv.at[:, lanes(c, HD)]),
+                lambda: to_sibling(4, down_hbm, down.at[c]),
+                lambda: to_sibling(5, qkv_hbm.at[:, query_at], w_q.at[c]),
+                lambda: to_sibling(6, placed_out, placed_in),
+                lambda: to_sibling(7, q_out, q3.at[:, c]),
+            )[i]()
+
         barrier = pltpu.get_barrier_semaphore()
 
         def greet(p, carry):
@@ -441,10 +470,12 @@
             return carry
 
         lax.fori_loop(1, groups, greet, 0)
-        for other in (*place.y_side, place.sibling):
-            pl.semaphore_signal(barrier, inc=1, device_id=other, device_id_type=MESH)
-
-        front = EncGather(place, buf, lambda block, h: block.at[pl.ds(2 * h, 2)], (fns, fnr, ffs, ffr, fgs, fgr))
+        for to in (*place.y_side, place.sibling):
+            pl.semaphore_signal(barrier, inc=1, device_id=to, device_id_type=MESH)
+
+        front = EncGather(
+            place, lambda y, c, h: buf.at[y, c, pl.ds(2 * h, 2)], (fns, fnr, ffs, ffr, fgs, fgr), shared=True
+        )
         values = p_ref[...].astype(jnp.float32)
         mean_square = jnp.mean(values * values, axis=1, keepdims=True)
         vision_rows = (values * lax.rsqrt(mean_square + EPSILON) * g_ref[...].reshape(1, vision)).astype(jnp.bfloat16)
@@ -458,13 +489,11 @@
         pl.semaphore_wait(barrier, groups - 1 + 3)
         front.start(0)
         front.start(1)
-        kv_columns = remote(
-            qkv_hbm.at[:, rest_at], w_kv.at[:, kv_at], place.sibling, c_send.at[0], c_recv.at[0]
-        )
-        kv_columns.start()
-        kv_bias[core] = qkv_bias_row[:, query_width:]
-        bias_columns = remote(kv_bias.at[core], kv_bias.at[core], place.sibling, c_send.at[1], c_recv.at[1])
-        bias_columns.start()
+        qkv_bias_of[core] = qb_ref[...].reshape(1, query_width + HD)
+        down_bias_of[core] = db_ref[...].reshape(1, width)
+        for i in range(4):
+            gift(i, core).start()
+        text_of[:, lanes(core, width)] = text_ref[tokens(core)]
 
         loads[0].wait()
         def turn(i, carry):
@@ -500,9 +529,12 @@
         both = jnp.dot(both.astype(jnp.bfloat16), spread_groups, preferred_element_type=jnp.float32)
         index = (lax.broadcasted_iota(jnp.int32, (1, slots), 1) % LMAX).astype(jnp.float32)
         target = jnp.where(index < both[8:9], both[:1] + index, -1.0)
-        token = lax.broadcasted_iota(jnp.int32, (rows, slots), 0).astype(jnp.float32)
-        placing = jnp.where(token == target, 1.0, 0.0)
-        covered = jnp.sum(placing, axis=1, keepdims=True) > 0.5
+        token = lax.broadcasted_iota(jnp.int32, (half, slots), 0)
+
+        def placing(c):
+            return jnp.where((token + c * half).astype(jnp.float32) == target, 1.0, 0.0)
+
+        covered = jnp.sum(placing(core), axis=1, keepdims=True) > 0.5
 
         def merge(*chips):
             grouped = jnp.concatenate(
@@ -523,6 +555,8 @@
         front.take(2)
         merge(place.ys[1], place.ys[2])
         front.finish_far()
+        for i in (4, 5):
+            gift(i, core).start()
         front.take(3)
         merge(place.ys[3])
 
@@ -538,25 +572,26 @@
 
         lax.fori_loop(1, groups, begin_swap, 0)
         inn[s] = out[s]
-        loads[1].wait()
-
         def end_swap(p, carry):
             swap(p, wrap(s + p, groups), wrap(s - p + groups, groups)).wait_recv()
             return carry
 
         lax.fori_loop(1, groups, end_swap, 0)
-        placed = jnp.dot(
-            placing.astype(jnp.bfloat16), inn[...].reshape(slots, units), preferred_element_type=jnp.float32
-        ).astype(jnp.bfloat16)
+        arrived = inn[...].reshape(slots, units)
+
+        def place_tokens(c):
+            return jnp.dot(
+                placing(c).astype(jnp.bfloat16), arrived, preferred_element_type=jnp.float32
+            ).astype(jnp.bfloat16)
+
+        placed_out[...] = place_tokens(other)
+        gift(6, core).start()
+        placed = place_tokens(core)
 
         targets = (place.ys[3], place.ys[2], place.ys[1], place.y)
 
-        def share(y_to, c_to):
-            start = pl.multiple_of((y_to * 2 + c_to) * width, width)
-            return jnp.dot(placed, down[:, pl.ds(start, width)], preferred_element_type=jnp.float32)
-
-        def pair(i):
-            return remote(sib_out.at[i], sib_in.at[i], place.sibling, p_send.at[i], p_recv.at[i])
+        def share(hidden_rows, c, y_to):
+            return jnp.dot(hidden_rows, down[c, :, lanes(y_to, wide)], preferred_element_type=jnp.float32)
 
         def relay(side):
             return remote(rel_out.at[side], rel_in.at[side], place.y_side[side], r_send.at[side], r_recv.at[side])
@@ -566,108 +601,108 @@
                 d_out.at[side, h], d_in.at[side, h], place.y_side[side], d_send.at[side, h], d_recv.at[side, h]
             )
 
-        halves = (slice(0, half), slice(half, rows))
+        halves = (slice(0, half // 2), slice(half // 2, half))
+        loads[1].wait()
         for i in range(4):
-            sib_out[i] = share(targets[i], 1 - core).astype(jnp.bfloat16)
-            pair(i).start()
+            own[i] = share(placed, core, targets[i])
+        gift(4, other).wait_recv()
+        gift(6, other).wait_recv()
         for i in range(4):
-            own[i] = share(targets[i], core)
-        pair(0).wait_recv()
-        for side in range(2):
-            at = halves[side]
-            rel_out[side] = (own[0, at] + sib_in[0, at].astype(jnp.float32)).astype(jnp.bfloat16)
-            relay(side).start()
-        for side in range(2):
-            pair(1 + side).wait_recv()
-            own[1 + side] = own[1 + side] + sib_in[1 + side].astype(jnp.float32)
-            d_out[side, 1 - side] = own[1 + side, halves[1 - side]].astype(jnp.bfloat16)
-            deliver(side, 1 - side).start()
-        pair(3).wait_recv()
-        own[3] = own[3] + sib_in[3].astype(jnp.float32) + db_ref[...].reshape(1, width)
+            own[i] = own[i] + share(placed_in[...], other, targets[i])
+            for side in range(2):
+                if i == 0:
+                    rel_out[side] = own[0, halves[side]].astype(jnp.bfloat16)
+                    relay(side).start()
+                if i == 1 + side:
+                    d_out[side, 1 - side] = own[i, halves[1 - side]].astype(jnp.bfloat16)
+                    deliver(side, 1 - side).start()
+        gift(1, other).wait_recv()
+        gift(2, other).wait_recv()
+        own[3] = own[3] + jnp.concatenate([down_bias_of[0], down_bias_of[1]], axis=1)
         for side in range(2):
             relay(side).wait_recv()
             d_out[side, side] = (own[1 + side, halves[side]] + rel_in[side].astype(jnp.float32)).astype(jnp.bfloat16)
             deliver(side, side).start()
 
-        token_id = lax.broadcasted_iota(jnp.int32, (rows, HD), 0) + s * rows
+        token_id = lax.broadcasted_iota(jnp.int32, (half, HD), 0) + s * rows + core * half
         sine, cosine = sine_cosine(token_id.astype(jnp.float32) * freq_ref[...])
-        signed = jnp.where(lax.broadcasted_iota(jnp.int32, (rows, HD), 1) < HD // 2, -sine, sine)
+        signed = jnp.where(lax.broadcasted_iota(jnp.int32, (half, HD), 1) < HD // 2, -sine, sine)
 
         def rotate(block):
             return block * cosine + pltpu.roll(block, HD // 2, 1) * signed
 
-        back = EncGather(place, full, lambda block, h: block.at[pl.ds(h * half, half)], (bns, bnr, bfs, bfr, bgs, bgr))
+        back = EncGather(
+            place, lambda y, c, h: full.at[y, pl.ds(h * (half // 2), half // 2)], (bns, bnr, bfs, bfr, None, None), shared=False
+        )
         for h in range(2):
             at = halves[h]
             total = own[3, at]
             for side in range(2):
                 deliver(side, h).wait_recv()
                 total = total + d_in[side, h].astype(jnp.float32)
-            kept = jnp.where(covered[at], total, text_ref[at].astype(jnp.float32))
-            full[place.y, core, at] = kept.astype(jnp.bfloat16)
+            kept = jnp.where(covered[at], total, text_of[at].astype(jnp.float32))
+            full[place.y, at] = kept.astype(jnp.bfloat16)
             back.start(h)
         squares[...] = jnp.zeros(squares.shape, jnp.float32)
 
         def add_squares(y):
-            for c in range(2):
-                block = full[y, c].astype(jnp.float32)
-                block = block * block
-                for g in range(width // HD):
-                    squares[...] += block[:, g * HD : (g + 1) * HD]
-
-        back.take(0)
+            block = full[y].astype(jnp.float32)
+            block = block * block
+            summed = block[:, :HD]
+            for g in range(1, wide // HD):
+                summed = summed + block[:, g * HD : (g + 1) * HD]
+            squares[...] += summed
+
         add_squares(place.ys[0])
         back.relay()
         back.finish_near()
         for i in range(1, 3):
-            back.take(i)
             add_squares(place.ys[i])
         back.finish_far()
-        back.take(3)
         add_squares(place.ys[3])
 
         scale = lax.rsqrt(jnp.sum(squares[...], axis=1, keepdims=True) * (1.0 / model) + EPSILON)
-        for block in range(blocks):
-            at = slice(block * width, (block + 1) * width)
-            normed[:, at] = (full[block // 2, block % 2].astype(jnp.float32) * scale * input_gain_row[:, at]).astype(
-                jnp.bfloat16
-            )
+        input_gain_row = gain_ref[...].reshape(1, model)
+        for y in range(ny):
+            at = slice(y * wide, (y + 1) * wide)
+            normed[:, at] = (full[y].astype(jnp.float32) * scale * input_gain_row[:, at]).astype(jnp.bfloat16)
         loads[2].wait()
-        remote(
-            qkv_hbm.at[:, rest_at], w_kv.at[:, other_at], place.sibling, c_send.at[0], c_recv.at[0]
-        ).wait_recv()
-        remote(kv_bias.at[core], kv_bias.at[1 - core], place.sibling, c_send.at[1], c_recv.at[1]).wait_recv()
+        gift(0, other).wait_recv()
+        gift(3, other).wait_recv()
         both = jnp.dot(normed[...], w_kv[...], preferred_element_type=jnp.float32)
-        key = rotate(both[:, :HD] + kv_bias[0]).T
+        key = rotate(both[:, :HD] + qkv_bias_of[0, :, query_width:]).T
         key_high = key.astype(jnp.bfloat16)
-        key_low = (key - key_high.astype(jnp.float32)).astype(jnp.bfloat16)
-        value = (both[:, HD:] + kv_bias[1]).astype(jnp.bfloat16)
-
-        for c in range(2):
-            @pl.when(core == c)
-            def _(c=c):
-                kv[z, c, x, :, :HD] = key_high[:, halves[c]]
-                kv[z, c, x, :, HD : 2 * HD] = key_low[:, halves[c]]
-                kv[z, c, x, :, 2 * HD :] = value[halves[c]]
+        kv[z, core, x, :, :HD] = key_high
+        kv[z, core, x, :, HD : 2 * HD] = (key - key_high.astype(jnp.float32)).astype(jnp.bfloat16)
+        kv[z, core, x, :, 2 * HD :] = (both[:, HD:] + qkv_bias_of[1, :, query_width:]).astype(jnp.bfloat16)
 
         plane = PlaneAttention(place, kv, q3, mx, den, acc, (xs, xr, hs, hr, zs, zr, ss, sr), nz, nx)
         plane.start()
 
+        scaling = HD ** (-0.5) * math.log2(math.e)
+
+        def project(c, store):
+            for first_head in range(0, heads, 2):
+                at = slice(first_head * HD, (first_head + 2) * HD)
+                query = jnp.dot(normed[...], w_q[c, :, at], preferred_element_type=jnp.float32) + qkv_bias_of[c, :, at]
+                for i in range(2):
+                    head = rotate(query[:, i * HD : (i + 1) * HD]) * scaling
+                    high = head.astype(jnp.bfloat16)
+                    low = (head - high.astype(jnp.float32)).astype(jnp.bfloat16)
+                    store(first_head + i, jnp.concatenate([high, high, low], axis=1))
+
+        def keep_out(h, value):
+            q_out[h] = value
+
+        def keep_here(h, value):
+            q3[h, core] = value
+
+        gift(5, other).wait_recv()
+        project(other, keep_out)
+        gift(7, core).start()
         loads[3].wait()
-        scaling = HD ** (-0.5) * math.log2(math.e)
-        for pair_of in range(heads // 2):
-            at = slice(pair_of * 2 * HD, (pair_of + 1) * 2 * HD)
-            query = jnp.dot(normed[...], w_q[:, at], preferred_element_type=jnp.float32) + qkv_bias_row[:, at]
-            for i in range(2):
-                rows_of = slice((pair_of * 2 + i) * rows, (pair_of * 2 + i + 1) * rows)
-                turned_query = rotate(query[:, i * HD : (i + 1) * HD]) * scaling
-                high = turned_query.astype(jnp.bfloat16)
-                q3[rows_of, :HD] = high
-                q3[rows_of, HD : 2 * HD] = high
-                q3[rows_of, 2 * HD :] = (turned_query - high.astype(jnp.float32)).astype(jnp.bfloat16)
-
-        plane.own_shard(key_high, key_low, value)
-        plane.run()
+        project(core, keep_here)
+        plane.run(lambda: gift(7, other).wait_recv())
         for h in range(heads):
             o_ref[:, h * HD : (h + 1) * HD] = plane.result(h).astype(o_ref.dtype)
 
@@ -678,10 +713,8 @@
         lax.fori_loop(1, groups, sent_swap, 0)
         front.drain()
         back.drain()
-        kv_columns.wait_send()
-        bias_columns.wait_send()
-        for i in range(4):
-            pair(i).wait_send()
+        for i in range(8):
+            gift(i, core).wait_send()
         for side in range(2):
             relay(side).wait_send()
             for h in range(2):
@@ -708,38 +741,39 @@
             pltpu.VMEM((ny, 2 * pad, units), bf16),
             pltpu.VMEM((groups, LMAX, units), bf16),
             pltpu.VMEM((groups, LMAX, units), bf16),
-            pltpu.VMEM(merge_down.shape, bf16),
-            pltpu.VMEM((model, query_width), bf16),
+            pltpu.VMEM((2, *merge_down.shape), bf16),
+            pltpu.VMEM((2, model, query_width), bf16),
             pltpu.VMEM((model, 2 * HD), bf16),
-            pltpu.VMEM((2, 1, HD), f32),
-            pltpu.VMEM((4, rows, width), bf16),
-            pltpu.VMEM((4, rows, width), bf16),
-            pltpu.VMEM((4, rows, width), f32),
-            pltpu.VMEM((2, half, width), bf16),
-            pltpu.VMEM((2, half, width), bf16),
-            pltpu.VMEM((2, 2, half, width), bf16),
-            pltpu.VMEM((2, 2, half, width), bf16),
-            pltpu.VMEM((ny, 2, rows, width), bf16),
-            pltpu.VMEM((rows, HD), f32),
-            pltpu.VMEM((rows, model), bf16),
+            pltpu.VMEM((2, 1, query_width + HD), f32),
+            pltpu.VMEM((2, 1, width), f32),
+            pltpu.VMEM((half, wide), bf16),
+            pltpu.VMEM((half, units), bf16),
+            pltpu.VMEM((half, units), bf16),
+            pltpu.VMEM((4, half, wide), f32),
+            pltpu.VMEM((2, half // 2, wide), bf16),
+            pltpu.VMEM((2, half // 2, wide), bf16),
+            pltpu.VMEM((2, 2, half // 2, wide), bf16),
+            pltpu.VMEM((2, 2, half // 2, wide), bf16),
+            pltpu.VMEM((ny, half, wide), bf16),
+            pltpu.VMEM((half, HD), f32),
+            pltpu.VMEM((half, model), bf16),
             pltpu.VMEM((nz, 2, nx, half, 3 * HD), bf16),
-            pltpu.VMEM((heads * rows, 3 * HD), bf16),
+            pltpu.VMEM((heads, 2, half, 3 * HD), bf16),
+            pltpu.VMEM((heads, half, 3 * HD), bf16),
             pltpu.VMEM((heads * rows, HD), f32),
             pltpu.VMEM((heads * rows, HD), f32),
             pltpu.VMEM((heads * rows, HD), f32),
             dma((4,)),
-            dma((2,)),
-            dma((2,)),
+            dma((8,)),
+            dma((8,)),
             dma((groups,)),
             dma((groups,)),
-            dma((4,)),
-            dma((4,)),
             dma((2,)),
             dma((2,)),
             dma((2, 2)),
             dma((2, 2)),
             *enc_sems,
-            *enc_sems,
+            *enc_sems[:4],
             dma((nz, 2)),
             dma((nz, 2)),
             dma((nz, 2)),

time: 98.8 us -> 97.8 us (0.990)
  no operation moved by 1% of the time
where the time goes in v3:
time: 97.8 us; the launch traced here: 97.3 us
  Pallas kernels  95.6 us (98%)
  local copies, waits for them, and re-layouts  1.67 us (2%)
    pallas_call x1, Pallas kernels, prefill(): pl.pallas_call(kernel, out_shape=jax.ShapeDtypeStruct((rows, query_width)...  95.6 us

profile of v3, /device:TPU:249, one launch (start us, length us, event | category | flops | bytes accessed | tf_op | source)
XLA Modules:
  0.0 97.3 jit_solution(2274248082058879928)
XLA Ops:
  0.0 95.6 %prefill.1 = bf16[256,512]{1,0:T(8,128)(2,1)} custom-call(bf16[112,1280]{1,0:T(8,128)(2,1)} %bitcast.5, f32[1280]{0:T(1024)} %g_ref.1, bf16[320,5120]{1,0:T(8,128)(2,1)} %bitcast.4, f32[320]{0:T(512)} %ub_ref.1, bf16[320,4096]{1,0:T(8,128)(2,1)} %down_hbm.1, f32[512]{0:T(512)} %db_ref.1, bf16[256,512]{1,0:T(8,128)(2,1)} %text_ref.1, s32[16,32]{1,0:T(8,128)} %bitcast.6, ...), custom_call_target="tpu_custom_call" | custom-call | tf_op jit(solution)/shard_map/prefill/pallas_call | solution.py:730
  95.6 1.7 %copy.15 = bf16[256,512]{1,0:T(8,128)(2,1)} copy(bf16[256,512]{1,0:T(8,128)(2,1)} %prefill.1) | data formatting | bytes 524288

commit v4 on v3

--- a/solution.py
+++ b/solution.py
@@ -190,40 +190,32 @@
             def _(side=side):
                 self.along_z(0, side, 0, 1).start()
 
-    def attend(self, high, low, v, restrict, fresh=False):
+    def compute(self, row, c, restrict=None):
+        block = self.kv[row, c]
+        high = jnp.concatenate([block[i, :, :HD] for i in range(self.nx)], axis=1)
+        low = jnp.concatenate([block[i, :, HD : 2 * HD] for i in range(self.nx)], axis=1)
+        v = block[:, :, 2 * HD :].reshape(self.nx * self.half, HD)
         stacked = jnp.concatenate([high, low, high], axis=0)
-        pieces = stacked.shape[1] // HD
-        parts = [slice(i, i + self.group) for i in range(0, self.heads * self.rows, self.group)]
         queries = [
             self.q3[h : h + self.together].reshape(self.group, 3 * HD) for h in range(0, self.heads, self.together)
         ]
         scores = [jnp.dot(query, stacked, preferred_element_type=jnp.float32) for query in queries]
-        for at, score in zip(parts, scores):
+        for i, score in enumerate(scores):
+            at = slice(i * self.group, (i + 1) * self.group)
             if restrict is not None:
-                score = jnp.concatenate([restrict(i, score[:, i * HD : (i + 1) * HD]) for i in range(pieces)], axis=1)
-            top = jnp.max(score, axis=1, keepdims=True)
-            new = jnp.broadcast_to(top, (self.group, HD)) if fresh else jnp.maximum(self.mx[at], top)
-            weights = jnp.exp2(score - jnp.concatenate([new] * pieces, axis=1))
+                score = jnp.concatenate([restrict(n, score[:, n * HD : (n + 1) * HD]) for n in range(self.nx)], axis=1)
+            new = jnp.maximum(self.mx[at], jnp.max(score, axis=1, keepdims=True))
+            weights = jnp.exp2(score - jnp.concatenate([new] * self.nx, axis=1))
             summed = weights[:, :HD]
-            for g in range(1, pieces):
-                summed = summed + weights[:, g * HD : (g + 1) * HD]
+            for n in range(1, self.nx):
+                summed = summed + weights[:, n * HD : (n + 1) * HD]
             product = jnp.dot(weights.astype(jnp.bfloat16), v, preferred_element_type=jnp.float32)
-            if fresh:
-                self.den[at] = summed
-                self.acc[at] = product
-            else:
-                factor = jnp.exp2(self.mx[at] - new)
-                self.den[at] = self.den[at] * factor + summed
-                self.acc[at] = self.acc[at] * factor + product
+            factor = jnp.exp2(self.mx[at] - new)
+            self.den[at] = self.den[at] * factor + summed
+            self.acc[at] = self.acc[at] * factor + product
             self.mx[at] = new
 
-    def compute(self, row, c, restrict=None, fresh=False):
-        block = self.kv[row, c]
-        high = jnp.concatenate([block[i, :, :HD] for i in range(self.nx)], axis=1)
-        low = jnp.concatenate([block[i, :, HD : 2 * HD] for i in range(self.nx)], axis=1)
-        self.attend(high, low, block[:, :, 2 * HD :].reshape(self.nx * self.half, HD), restrict, fresh)
-
-    def own_row(self, c, fresh):
+    def own_row(self, c):
         x = self.place.x
         shape = (self.group, HD)
         token = lax.broadcasted_iota(jnp.int32, shape, 0) & (self.rows - 1)
@@ -233,19 +225,7 @@
             limit = jnp.where(x > i, 2 * self.rows, jnp.where(x == i, 0, -2 * self.rows)) - c * self.half
             return jnp.where(ahead <= limit, piece, NEG)
 
-        self.compute(self.place.z, c, restrict, fresh)
-
-    def far_rows(self, k, c):
-        def step(i, carry):
-            row = wrap(self.place.z + k * (2 * i - 1), self.nz)
-
-            @pl.when(row < self.place.z)
-            def _():
-                self.compute(row, c)
-
-            return carry
-
-        lax.fori_loop(0, len(self.ring_rows(k)), step, 0)
+        self.compute(self.place.z, c, restrict)
 
     def pass_rows(self, k, chosen):
         far = self.far
@@ -343,21 +323,48 @@
                 self.give(j).start()
 
     def run(self, queries_here):
-        core, far = self.place.core, self.far
-        for t in range(1, far + 4):
-            self.early(t)
-            if t > 3:
-                self.from_sibling(t - 3)
-                self.far_rows(t - 3, 1 - core)
-            self.late(t)
-            if t == 3:
-                self.from_sibling(0)
-                self.own_row(1 - core, False)
-            if t == 2:
-                queries_here()
-                self.own_row(core, True)
-            elif 3 <= t <= far + 2:
-                self.far_rows(t - 2, core)
+        core, far, z, nz = self.place.core, self.far, self.place.z, self.nz
+        self.mx[...] = jnp.full(self.mx.shape, NEG, jnp.float32)
+        self.den[...] = jnp.zeros(self.den.shape, jnp.float32)
+        self.acc[...] = jnp.zeros(self.acc.shape, jnp.float32)
+
+        def phase(i, carry):
+            for t in range(1, far + 4):
+                @pl.when(i == 2 * t - 2)
+                def _(t=t):
+                    self.early(t)
+                    if t > 3:
+                        self.from_sibling(t - 3)
+
+                @pl.when(i == 2 * t - 1)
+                def _(t=t):
+                    self.late(t)
+                    if t == 2:
+                        queries_here()
+                    if t == 3:
+                        self.from_sibling(0)
+
+            @pl.when((i == 3) | (i == 5))
+            def _():
+                self.own_row(jnp.where(i == 3, core, 1 - core))
+
+            odd = lax.rem(i, 2)
+            k = lax.div(i, 2) - 2 + odd
+            c = jnp.where(odd == 1, core, 1 - core)
+
+            def attend(n, inner):
+                row = wrap(z + k * (2 * n - 1), nz)
+
+                @pl.when((k >= 1) & (k <= far) & (row < z) & ((k < far) | (n == 0)))
+                def _():
+                    self.compute(row, c)
+
+                return inner
+
+            lax.fori_loop(0, 2, attend, 0)
+            return carry
+
+        lax.fori_loop(0, 2 * (far + 3), phase, 0)
 
     def result(self, h):
         at = slice(h * self.rows, (h + 1) * self.rows)
@@ -405,6 +412,7 @@
 ):
     patch_rows, vision = patches.shape
     units, joined = up_t.shape
+    padded = -(-units // HD) * HD
     part = patch_rows // 4
     pad = -(-part // 16) * 16
     blocks = 2 * ny
@@ -421,8 +429,8 @@
     def kernel(
         p_ref, g_ref, up_hbm, ub_ref, down_hbm, db_ref, text_ref, len_s, off_s, len_v, off_v, gain_ref, qkv_hbm, qb_ref,
         freq_ref, o_ref,
-        buf, turned, up, hid, out, inn, down, w_q, w_kv, qkv_bias_of, down_bias_of, text_of, placed_out, placed_in,
-        own, rel_out, rel_in, d_out, d_in, full, squares, normed, kv, q3, q_out, mx, den, acc,
+        buf, turned, up, hid, out, inn, down, w_q, w_kv, qkv_bias_of, down_bias_of, text_of, placed_out, placed_in, placed_mine,
+        merged_sum, turn_cos, turn_sin, gain_row, own, rel_out, rel_in, d_out, d_in, full, squares, normed, kv, q3, mx, den, acc,
         w_sem, c_send, c_recv, a_send, a_recv, r_send, r_recv, d_send, d_recv,
         fns, fnr, ffs, ffr, fgs, fgr, bns, bnr, bfs, bfr,
         xs, xr, hs, hr, zs, zr, ss, sr,
@@ -443,7 +451,7 @@
             pltpu.make_async_copy(up_hbm, turned, w_sem.at[0]),
             pltpu.make_async_copy(down_hbm, down.at[core], w_sem.at[1]),
             pltpu.make_async_copy(qkv_hbm.at[:, rest_at], w_kv.at[:, lanes(core, HD)], w_sem.at[2]),
-            pltpu.make_async_copy(qkv_hbm.at[:, query_at], w_q.at[core], w_sem.at[3]),
+            pltpu.make_async_copy(qkv_hbm.at[:, query_at], w_q, w_sem.at[3]),
         )
         for load in loads:
             load.start()
@@ -458,9 +466,8 @@
                 lambda: to_sibling(2, text_ref.at[tokens(other)], text_of.at[:, lanes(c, width)]),
                 lambda: to_sibling(3, qkv_hbm.at[:, rest_at], w_kv.at[:, lanes(c, HD)]),
                 lambda: to_sibling(4, down_hbm, down.at[c]),
-                lambda: to_sibling(5, qkv_hbm.at[:, query_at], w_q.at[c]),
+                lambda: to_sibling(5, normed.at[core], normed.at[c]),
                 lambda: to_sibling(6, placed_out, placed_in),
-                lambda: to_sibling(7, q_out, q3.at[:, c]),
             )[i]()
 
         barrier = pltpu.get_barrier_semaphore()
@@ -491,7 +498,7 @@
         front.start(1)
         qkv_bias_of[core] = qb_ref[...].reshape(1, query_width + HD)
         down_bias_of[core] = db_ref[...].reshape(1, width)
-        for i in range(4):
+        for i in range(5):
             gift(i, core).start()
         text_of[:, lanes(core, width)] = text_ref[tokens(core)]
 
@@ -536,15 +543,20 @@
 
         covered = jnp.sum(placing(core), axis=1, keepdims=True) > 0.5
 
+        out[...] = jnp.zeros(out.shape, jnp.bfloat16)
+
         def merge(*chips):
-            grouped = jnp.concatenate(
-                [
-                    jnp.concatenate([buf[y, :, q].reshape(2 * pad, vision) for q in range(4)], axis=1)
-                    for y in chips
-                ],
-                axis=0,
-            )
-            inner = jnp.dot(grouped, up[...], preferred_element_type=jnp.float32) + ub_ref[...].reshape(1, units)
+            count = len(chips) * 2 * pad
+            merged_sum[:count] = jnp.broadcast_to(ub_ref[...].reshape(1, units), (count, units))
+
+            def add_part(q, carry):
+                grouped = jnp.concatenate([buf[y, :, q].reshape(2 * pad, vision) for y in chips], axis=0)
+                weights = up[pl.ds(pl.multiple_of(q * vision, vision), vision), :]
+                merged_sum[:count] += jnp.dot(grouped, weights, preferred_element_type=jnp.float32)
+                return carry
+
+            lax.fori_loop(0, 4, add_part, 0)
+            inner = merged_sum[:count]
             inner = (0.5 * inner * (1.0 + lax.erf(inner * math.sqrt(0.5)))).astype(jnp.bfloat16)
             for i, y in enumerate(chips):
                 hid[y] = inner[i * 2 * pad : (i + 1) * 2 * pad]
@@ -555,13 +567,11 @@
         front.take(2)
         merge(place.ys[1], place.ys[2])
         front.finish_far()
-        for i in (4, 5):
-            gift(i, core).start()
         front.take(3)
         merge(place.ys[3])
 
         chosen = jnp.dot(pick, hid[...].reshape(blocks * pad, units), preferred_element_type=jnp.float32)
-        out[...] = chosen.astype(jnp.bfloat16).reshape(groups, LMAX, units)
+        out[:, :, :units] = chosen.astype(jnp.bfloat16).reshape(groups, LMAX, units)
 
         def swap(p, at, arrives):
             return remote(out.at[at], inn.at[arrives], (e, at), a_send.at[p], a_recv.at[p])
@@ -577,7 +587,7 @@
             return carry
 
         lax.fori_loop(1, groups, end_swap, 0)
-        arrived = inn[...].reshape(slots, units)
+        arrived = inn[:, :, :units].reshape(slots, units)
 
         def place_tokens(c):
             return jnp.dot(
@@ -586,9 +596,7 @@
 
         placed_out[...] = place_tokens(other)
         gift(6, core).start()
-        placed = place_tokens(core)
-
-        targets = (place.ys[3], place.ys[2], place.ys[1], place.y)
+        placed_mine[...] = place_tokens(core)
 
         def share(hidden_rows, c, y_to):
             return jnp.dot(hidden_rows, down[c, :, lanes(y_to, wide)], preferred_element_type=jnp.float32)
@@ -603,12 +611,22 @@
 
         halves = (slice(0, half // 2), slice(half // 2, half))
         loads[1].wait()
-        for i in range(4):
-            own[i] = share(placed, core, targets[i])
+        def target(i):
+            return wrap(place.y + jnp.where(i == 0, 2, jnp.where(i == 1, 1, jnp.where(i == 2, -1, 0))), ny)
+
+        def add_own(i, carry):
+            own[i] = share(placed_mine[...], core, target(i))
+            return carry
+
+        def add_other(i, carry):
+            own[i] += share(placed_in[...], other, target(i))
+            return carry
+
+        lax.fori_loop(0, 4, add_own, 0)
         gift(4, other).wait_recv()
         gift(6, other).wait_recv()
-        for i in range(4):
-            own[i] = own[i] + share(placed_in[...], other, targets[i])
+        for i in range(3):
+            lax.fori_loop(i, i + 1 if i < 2 else 4, add_other, 0)
             for side in range(2):
                 if i == 0:
                     rel_out[side] = own[0, halves[side]].astype(jnp.bfloat16)
@@ -624,12 +642,14 @@
             d_out[side, side] = (own[1 + side, halves[side]] + rel_in[side].astype(jnp.float32)).astype(jnp.bfloat16)
             deliver(side, side).start()
 
-        token_id = lax.broadcasted_iota(jnp.int32, (half, HD), 0) + s * rows + core * half
-        sine, cosine = sine_cosine(token_id.astype(jnp.float32) * freq_ref[...])
-        signed = jnp.where(lax.broadcasted_iota(jnp.int32, (half, HD), 1) < HD // 2, -sine, sine)
-
-        def rotate(block):
-            return block * cosine + pltpu.roll(block, HD // 2, 1) * signed
+        for c in range(2):
+            token_id = lax.broadcasted_iota(jnp.int32, (half, HD), 0) + s * rows + c * half
+            sine, cosine = sine_cosine(token_id.astype(jnp.float32) * freq_ref[...])
+            turn_cos[c] = cosine
+            turn_sin[c] = jnp.where(lax.broadcasted_iota(jnp.int32, (half, HD), 1) < HD // 2, -sine, sine)
+
+        def rotate(block, c):
+            return block * turn_cos[c] + pltpu.roll(block, HD // 2, 1) * turn_sin[c]
 
         back = EncGather(
             place, lambda y, c, h: full.at[y, pl.ds(h * (half // 2), half // 2)], (bns, bnr, bfs, bfr, None, None), shared=False
@@ -662,15 +682,20 @@
         add_squares(place.ys[3])
 
         scale = lax.rsqrt(jnp.sum(squares[...], axis=1, keepdims=True) * (1.0 / model) + EPSILON)
-        input_gain_row = gain_ref[...].reshape(1, model)
-        for y in range(ny):
-            at = slice(y * wide, (y + 1) * wide)
-            normed[:, at] = (full[y].astype(jnp.float32) * scale * input_gain_row[:, at]).astype(jnp.bfloat16)
+        gain_row[...] = gain_ref[...].reshape(1, model)
+
+        def norm_part(y, carry):
+            at = lanes(y, wide)
+            normed[core, :, at] = (full[y].astype(jnp.float32) * scale * gain_row[:, at]).astype(jnp.bfloat16)
+            return carry
+
+        lax.fori_loop(0, ny, norm_part, 0)
+        gift(5, core).start()
         loads[2].wait()
         gift(0, other).wait_recv()
         gift(3, other).wait_recv()
-        both = jnp.dot(normed[...], w_kv[...], preferred_element_type=jnp.float32)
-        key = rotate(both[:, :HD] + qkv_bias_of[0, :, query_width:]).T
+        both = jnp.dot(normed[core], w_kv[...], preferred_element_type=jnp.float32)
+        key = rotate(both[:, :HD] + qkv_bias_of[0, :, query_width:], core).T
         key_high = key.astype(jnp.bfloat16)
         kv[z, core, x, :, :HD] = key_high
         kv[z, core, x, :, HD : 2 * HD] = (key - key_high.astype(jnp.float32)).astype(jnp.bfloat16)
@@ -680,29 +705,30 @@
         plane.start()
 
         scaling = HD ** (-0.5) * math.log2(math.e)
-
-        def project(c, store):
-            for first_head in range(0, heads, 2):
-                at = slice(first_head * HD, (first_head + 2) * HD)
-                query = jnp.dot(normed[...], w_q[c, :, at], preferred_element_type=jnp.float32) + qkv_bias_of[c, :, at]
-                for i in range(2):
-                    head = rotate(query[:, i * HD : (i + 1) * HD]) * scaling
-                    high = head.astype(jnp.bfloat16)
-                    low = (head - high.astype(jnp.float32)).astype(jnp.bfloat16)
-                    store(first_head + i, jnp.concatenate([high, high, low], axis=1))
-
-        def keep_out(h, value):
-            q_out[h] = value
-
-        def keep_here(h, value):
-            q3[h, core] = value
-
-        gift(5, other).wait_recv()
-        project(other, keep_out)
-        gift(7, core).start()
         loads[3].wait()
-        project(core, keep_here)
-        plane.run(lambda: gift(7, other).wait_recv())
+
+        def project(i, carry):
+            pairs = heads // 2
+            c = jnp.where(i < pairs, core, other)
+            first_head = 2 * lax.rem(i, pairs)
+
+            @pl.when(i == pairs)
+            def _():
+                gift(5, other).wait_recv()
+
+            at = pl.ds(pl.multiple_of(first_head * HD, 2 * HD), 2 * HD)
+            query = jnp.dot(normed[c], w_q[:, at], preferred_element_type=jnp.float32) + qkv_bias_of[core, :, at]
+            for n in range(2):
+                head = rotate(query[:, n * HD : (n + 1) * HD], c) * scaling
+                high = head.astype(jnp.bfloat16)
+                low = (head - high.astype(jnp.float32)).astype(jnp.bfloat16)
+                q3[first_head + n, c, :, :HD] = high
+                q3[first_head + n, c, :, HD : 2 * HD] = high
+                q3[first_head + n, c, :, 2 * HD :] = low
+            return carry
+
+        lax.fori_loop(0, heads, project, 0)
+        plane.run(lambda: None)
         for h in range(heads):
             o_ref[:, h * HD : (h + 1) * HD] = plane.result(h).astype(o_ref.dtype)
 
@@ -713,7 +739,7 @@
         lax.fori_loop(1, groups, sent_swap, 0)
         front.drain()
         back.drain()
-        for i in range(8):
+        for i in range(7):
             gift(i, core).wait_send()
         for side in range(2):
             relay(side).wait_send()
@@ -739,16 +765,21 @@
             pltpu.VMEM((units, joined), bf16),
             pltpu.VMEM((joined, units), bf16),
             pltpu.VMEM((ny, 2 * pad, units), bf16),
-            pltpu.VMEM((groups, LMAX, units), bf16),
-            pltpu.VMEM((groups, LMAX, units), bf16),
+            pltpu.VMEM((groups, LMAX, padded), bf16),
+            pltpu.VMEM((groups, LMAX, padded), bf16),
             pltpu.VMEM((2, *merge_down.shape), bf16),
-            pltpu.VMEM((2, model, query_width), bf16),
+            pltpu.VMEM((model, query_width), bf16),
             pltpu.VMEM((model, 2 * HD), bf16),
             pltpu.VMEM((2, 1, query_width + HD), f32),
             pltpu.VMEM((2, 1, width), f32),
             pltpu.VMEM((half, wide), bf16),
             pltpu.VMEM((half, units), bf16),
             pltpu.VMEM((half, units), bf16),
+            pltpu.VMEM((half, units), bf16),
+            pltpu.VMEM((4 * pad, units), f32),
+            pltpu.VMEM((2, half, HD), f32),
+            pltpu.VMEM((2, half, HD), f32),
+            pltpu.VMEM((1, model), f32),
             pltpu.VMEM((4, half, wide), f32),
             pltpu.VMEM((2, half // 2, wide), bf16),
             pltpu.VMEM((2, half // 2, wide), bf16),
@@ -756,16 +787,15 @@
             pltpu.VMEM((2, 2, half // 2, wide), bf16),
             pltpu.VMEM((ny, half, wide), bf16),
             pltpu.VMEM((half, HD), f32),
-            pltpu.VMEM((half, model), bf16),
+            pltpu.VMEM((2, half, model), bf16),
             pltpu.VMEM((nz, 2, nx, half, 3 * HD), bf16),
             pltpu.VMEM((heads, 2, half, 3 * HD), bf16),
-            pltpu.VMEM((heads, half, 3 * HD), bf16),
             pltpu.VMEM((heads * rows, HD), f32),
             pltpu.VMEM((heads * rows, HD), f32),
             pltpu.VMEM((heads * rows, HD), f32),
             dma((4,)),
-            dma((8,)),
-            dma((8,)),
+            dma((7,)),
+            dma((7,)),
             dma((groups,)),
             dma((groups,)),
             dma((2,)),

time: 97.8 us -> 98.7 us (level)
  Pallas kernels: 95.6 us -> 96.9 us
    pallas_call x1, Pallas kernels: 95.6 us -> 96.9 us  [prefill(): pl.pallas_call(kernel, out_shape=jax.ShapeDtypeStruct((rows, query_width)...]
where the time goes in v4:
time: 98.7 us; the launch traced here: 98.6 us
  Pallas kernels  96.9 us (98%)
  local copies, waits for them, and re-layouts  1.67 us (2%)
    pallas_call x1, Pallas kernels, prefill(): pl.pallas_call(kernel, out_shape=jax.ShapeDtypeStruct((rows, query_width)...  96.9 us

profile of v4, /device:TPU:249, one launch (start us, length us, event | category | flops | bytes accessed | tf_op | source)
XLA Modules:
  0.0 98.6 jit_solution(1486328053774201393)
XLA Ops:
  0.0 96.9 %prefill.1 = bf16[256,512]{1,0:T(8,128)(2,1)} custom-call(bf16[112,1280]{1,0:T(8,128)(2,1)} %bitcast.5, f32[1280]{0:T(1024)} %g_ref.1, bf16[320,5120]{1,0:T(8,128)(2,1)} %bitcast.4, f32[320]{0:T(512)} %ub_ref.1, bf16[320,4096]{1,0:T(8,128)(2,1)} %down_hbm.1, f32[512]{0:T(512)} %db_ref.1, bf16[256,512]{1,0:T(8,128)(2,1)} %text_ref.1, s32[16,32]{1,0:T(8,128)} %bitcast.6, ...), custom_call_target="tpu_custom_call" | custom-call | tf_op jit(solution)/shard_map/prefill/pallas_call | solution.py:756
  96.9 1.7 %copy.15 = bf16[256,512]{1,0:T(8,128)(2,1)} copy(bf16[256,512]{1,0:T(8,128)(2,1)} %prefill.1) | data formatting | bytes 524288

commit v5 on v4

--- a/solution.py
+++ b/solution.py
@@ -260,7 +260,8 @@
                         @pl.when(self.goes(direction, 1))
                         def _(side=side, direction=direction):
                             self.along_z(0, direction, 1 + side, 1).start()
-            self.pass_rows(t - 2, (0, 1))
+            self.pass_rows(t - 2, (1,))
+            self.pass_rows(t - 1, (0,))
 
         @pl.when(self.place.core == 1)
         def _():
@@ -339,7 +340,7 @@
                 @pl.when(i == 2 * t - 1)
                 def _(t=t):
                     self.late(t)
-                    if t == 2:
+                    if t == 1:
                         queries_here()
                     if t == 3:
                         self.from_sibling(0)
@@ -412,9 +413,9 @@
 ):
     patch_rows, vision = patches.shape
     units, joined = up_t.shape
-    padded = -(-units // HD) * HD
     part = patch_rows // 4
     pad = -(-part // 16) * 16
+    cut = -(-patch_rows // 32) * 16
     blocks = 2 * ny
     wide = 2 * text.shape[1]
     groups = nz * nx
@@ -429,7 +430,7 @@
     def kernel(
         p_ref, g_ref, up_hbm, ub_ref, down_hbm, db_ref, text_ref, len_s, off_s, len_v, off_v, gain_ref, qkv_hbm, qb_ref,
         freq_ref, o_ref,
-        buf, turned, up, hid, out, inn, down, w_q, w_kv, qkv_bias_of, down_bias_of, text_of, placed_out, placed_in, placed_mine,
+        buf, order, ordered, turned, up, hid, out, inn, down, w_q, w_kv, qkv_bias_of, down_bias_of, text_of, placed_out, placed_in, placed_mine,
         merged_sum, turn_cos, turn_sin, gain_row, own, rel_out, rel_in, d_out, d_in, full, squares, normed, kv, q3, mx, den, acc,
         w_sem, c_send, c_recv, a_send, a_recv, r_send, r_recv, d_send, d_recv,
         fns, fnr, ffs, ffr, fgs, fgr, bns, bnr, bfs, bfr,
@@ -481,18 +482,13 @@
             pl.semaphore_signal(barrier, inc=1, device_id=to, device_id_type=MESH)
 
         front = EncGather(
-            place, lambda y, c, h: buf.at[y, c, pl.ds(2 * h, 2)], (fns, fnr, ffs, ffr, fgs, fgr), shared=True
+            place, lambda y, c, h: buf.at[y, c, pl.ds(h * cut, patch_rows - cut if h else cut)], (fns, fnr, ffs, ffr, fgs, fgr), shared=True
         )
         values = p_ref[...].astype(jnp.float32)
         mean_square = jnp.mean(values * values, axis=1, keepdims=True)
-        vision_rows = (values * lax.rsqrt(mean_square + EPSILON) * g_ref[...].reshape(1, vision)).astype(jnp.bfloat16)
-        to = lax.broadcasted_iota(jnp.int32, (4 * pad, patch_rows), 0)
-        source = lax.broadcasted_iota(jnp.int32, (4 * pad, patch_rows), 1)
-        moved = (source == 4 * (to % pad) + to // pad) & (to % pad < part)
-        order = jnp.where(moved, 1.0, 0.0).astype(jnp.bfloat16)
-        sorted_rows = jnp.dot(order, vision_rows, preferred_element_type=jnp.float32).astype(jnp.bfloat16)
-        for q in range(4):
-            buf[place.y, core, q] = sorted_rows[q * pad : (q + 1) * pad]
+        buf[place.y, core] = (
+            values * lax.rsqrt(mean_square + EPSILON) * g_ref[...].reshape(1, vision)
+        ).astype(jnp.bfloat16)
         pl.semaphore_wait(barrier, groups - 1 + 3)
         front.start(0)
         front.start(1)
@@ -513,6 +509,11 @@
         front.relay()
         lax.fori_loop(turns // 2, turns, turn, 0)
         front.finish_near()
+
+        to = lax.broadcasted_iota(jnp.int32, (4 * pad, patch_rows), 0)
+        source = lax.broadcasted_iota(jnp.int32, (4 * pad, patch_rows), 1)
+        moved = (source == 4 * (to % pad) + to // pad) & (to % pad < part)
+        order[...] = jnp.where(moved, 1.0, 0.0).astype(jnp.bfloat16)
 
         lane = lax.broadcasted_iota(jnp.int32, (1, blocks * pad), 1)
         merged = jnp.where(lane % pad < part, lane // pad * part + lane % pad, -1)
@@ -543,14 +544,20 @@
 
         covered = jnp.sum(placing(core), axis=1, keepdims=True) > 0.5
 
-        out[...] = jnp.zeros(out.shape, jnp.bfloat16)
-
         def merge(*chips):
             count = len(chips) * 2 * pad
+
+            def sort(c, carry):
+                for i, y in enumerate(chips):
+                    rows_of = jnp.dot(order[...], buf[y, c], preferred_element_type=jnp.float32)
+                    ordered[:, i, c] = rows_of.astype(jnp.bfloat16).reshape(4, pad, vision)
+                return carry
+
+            lax.fori_loop(0, 2, sort, 0)
             merged_sum[:count] = jnp.broadcast_to(ub_ref[...].reshape(1, units), (count, units))
 
             def add_part(q, carry):
-                grouped = jnp.concatenate([buf[y, :, q].reshape(2 * pad, vision) for y in chips], axis=0)
+                grouped = ordered[q, : len(chips)].reshape(count, vision)
                 weights = up[pl.ds(pl.multiple_of(q * vision, vision), vision), :]
                 merged_sum[:count] += jnp.dot(grouped, weights, preferred_element_type=jnp.float32)
                 return carry
@@ -571,7 +578,7 @@
         merge(place.ys[3])
 
         chosen = jnp.dot(pick, hid[...].reshape(blocks * pad, units), preferred_element_type=jnp.float32)
-        out[:, :, :units] = chosen.astype(jnp.bfloat16).reshape(groups, LMAX, units)
+        out[...] = chosen.astype(jnp.bfloat16).reshape(groups, LMAX, units)
 
         def swap(p, at, arrives):
             return remote(out.at[at], inn.at[arrives], (e, at), a_send.at[p], a_recv.at[p])
@@ -587,7 +594,7 @@
             return carry
 
         lax.fori_loop(1, groups, end_swap, 0)
-        arrived = inn[:, :, :units].reshape(slots, units)
+        arrived = inn[...].reshape(slots, units)
 
         def place_tokens(c):
             return jnp.dot(
@@ -712,10 +719,6 @@
             c = jnp.where(i < pairs, core, other)
             first_head = 2 * lax.rem(i, pairs)
 
-            @pl.when(i == pairs)
-            def _():
-                gift(5, other).wait_recv()
-
             at = pl.ds(pl.multiple_of(first_head * HD, 2 * HD), 2 * HD)
             query = jnp.dot(normed[c], w_q[:, at], preferred_element_type=jnp.float32) + qkv_bias_of[core, :, at]
             for n in range(2):
@@ -727,8 +730,12 @@
                 q3[first_head + n, c, :, 2 * HD :] = low
             return carry
 
-        lax.fori_loop(0, heads, project, 0)
-        plane.run(lambda: None)
+        def sibling_tokens():
+            gift(5, other).wait_recv()
+            lax.fori_loop(heads // 2, heads, project, 0)
+
+        lax.fori_loop(0, heads // 2, project, 0)
+        plane.run(sibling_tokens)
         for h in range(heads):
             o_ref[:, h * HD : (h + 1) * HD] = plane.result(h).astype(o_ref.dtype)
 
@@ -761,12 +768,14 @@
         ],
         out_specs=vmem,
         scratch_shapes=[
-            pltpu.VMEM((ny, 2, 4, pad, vision), bf16),
+            pltpu.VMEM((ny, 2, patch_rows, vision), bf16),
+            pltpu.VMEM((4 * pad, patch_rows), bf16),
+            pltpu.VMEM((4, 2, 2, pad, vision), bf16),
             pltpu.VMEM((units, joined), bf16),
             pltpu.VMEM((joined, units), bf16),
             pltpu.VMEM((ny, 2 * pad, units), bf16),
-            pltpu.VMEM((groups, LMAX, padded), bf16),
-            pltpu.VMEM((groups, LMAX, padded), bf16),
+            pltpu.VMEM((groups, LMAX, units), bf16),
+            pltpu.VMEM((groups, LMAX, units), bf16),
             pltpu.VMEM((2, *merge_down.shape), bf16),
             pltpu.VMEM((model, query_width), bf16),
             pltpu.VMEM((model, 2 * HD), bf16),

time: 98.7 us -> 97.9 us (level)
  no operation moved by 1% of the time
where the time goes in v5:
time: 97.9 us; the launch traced here: 97.7 us
  Pallas kernels  96.1 us (98%)
  local copies, waits for them, and re-layouts  1.67 us (2%)
    pallas_call x1, Pallas kernels, prefill(): pl.pallas_call(kernel, out_shape=jax.ShapeDtypeStruct((rows, query_width)...  96.1 us

profile of v5, /device:TPU:249, one launch (start us, length us, event | category | flops | bytes accessed | tf_op | source)
XLA Modules:
  0.0 97.7 jit_solution(14669647526084914477)
XLA Ops:
  0.0 96.1 %prefill.1 = bf16[256,512]{1,0:T(8,128)(2,1)} custom-call(bf16[112,1280]{1,0:T(8,128)(2,1)} %bitcast.5, f32[1280]{0:T(1024)} %g_ref.1, bf16[320,5120]{1,0:T(8,128)(2,1)} %bitcast.4, f32[320]{0:T(512)} %ub_ref.1, bf16[320,4096]{1,0:T(8,128)(2,1)} %down_hbm.1, f32[512]{0:T(512)} %db_ref.1, bf16[256,512]{1,0:T(8,128)(2,1)} %text_ref.1, s32[16,32]{1,0:T(8,128)} %bitcast.6, ...), custom_call_target="tpu_custom_call" | custom-call | tf_op jit(solution)/shard_map/prefill/pallas_call | solution.py:763
  96.1 1.7 %copy.15 = bf16[256,512]{1,0:T(8,128)(2,1)} copy(bf16[256,512]{1,0:T(8,128)(2,1)} %prefill.1) | data formatting | bytes 524288

commit v6 on v5

--- a/solution.py
+++ b/solution.py
@@ -228,72 +228,67 @@
         self.compute(self.place.z, c, restrict)
 
     def pass_rows(self, k, chosen):
-        far = self.far
-        if not 1 <= k <= far:
+        if not 1 <= k < self.far:
             return
         for side in range(2):
-            j = min(2 * k - 1 + side, 2 * far - 1)
-            mine = [i for i in chosen if k < far or i // 2 == side]
-            onward = [i for i in chosen if k + 1 < far or (k + 1 == far and i // 2 == side)]
+            j = 2 * k - 1 + side
 
             @pl.when(self.comes(side, k))
-            def _(side=side, j=j, mine=mine):
-                for i in mine:
+            def _(side=side, j=j):
+                for i in chosen:
                     self.along_z(j, side, i, k).wait_recv()
 
-            if onward:
+            if k + 1 < self.far:
                 @pl.when(self.goes(side, k + 1))
-                def _(side=side, j=j, onward=onward):
-                    for i in onward:
+                def _(side=side, j=j):
+                    for i in chosen:
                         self.along_z(j, side, i, k + 1).start()
+
+    def spreads(self, j):
+        everyone = j in (0, 2 * self.far - 1)
+        return self.needed(j) if everyone else self.needed(j) & (self.place.core == 1)
 
     def early(self, t):
         far = self.far
+        if 1 <= t <= far:
+            for side in range(2):
+                j = min(2 * t - 1 + side, 2 * far - 1)
+
+                @pl.when(self.comes(side, t))
+                def _(side=side, j=j):
+                    if t < far:
+                        self.along_z(j, side, 0, t).wait_recv()
+                    else:
+                        self.half_along_z(j, side).wait_recv()
+
+                if t < far:
+                    @pl.when(self.goes(side, t + 1))
+                    def _(side=side, j=j):
+                        if t + 1 < far:
+                            self.along_z(j, side, 0, t + 1).start()
+                        else:
+                            self.half_along_z(j, side).start()
+            for j in self.ring_rows(t):
+                @pl.when(self.spreads(j))
+                def _(j=j):
+                    for side in range(2):
+                        self.along_x(j, side, 0).start()
+        for j in self.ring_rows(t - 1):
+            @pl.when(self.spreads(j))
+            def _(j=j):
+                for side in range(2):
+                    self.along_x(j, side, 1 + side).wait_recv()
+                    self.half_on(j, side, 1 + side).start()
 
         @pl.when(self.place.core == 0)
         def _():
             if t == 1:
-                for side in range(2):
-                    self.along_x(0, side, 1 + side).wait_recv()
-                    self.half_on(0, side, 1 + side).start()
-                    for direction in range(2):
-                        @pl.when(self.goes(direction, 1))
-                        def _(side=side, direction=direction):
-                            self.along_z(0, direction, 1 + side, 1).start()
+                for direction in range(2):
+                    @pl.when(self.goes(direction, 1))
+                    def _(direction=direction):
+                        for i in (1, 2):
+                            self.along_z(0, direction, i, 1).start()
             self.pass_rows(t - 2, (1,))
-            self.pass_rows(t - 1, (0,))
-
-        @pl.when(self.place.core == 1)
-        def _():
-            if 1 <= t <= far:
-                for side in range(2):
-                    j = min(2 * t - 1 + side, 2 * far - 1)
-
-                    @pl.when(self.comes(side, t))
-                    def _(side=side, j=j):
-                        if t < far:
-                            self.along_z(j, side, 0, t).wait_recv()
-                        else:
-                            self.half_along_z(j, side).wait_recv()
-
-                    if t < far:
-                        @pl.when(self.goes(side, t + 1))
-                        def _(side=side, j=j):
-                            if t + 1 < far:
-                                self.along_z(j, side, 0, t + 1).start()
-                            else:
-                                self.half_along_z(j, side).start()
-                for j in self.ring_rows(t):
-                    @pl.when(self.needed(j))
-                    def _(j=j):
-                        for side in range(2):
-                            self.along_x(j, side, 0).start()
-            for j in self.ring_rows(t - 1):
-                @pl.when(self.needed(j))
-                def _(j=j):
-                    for side in range(2):
-                        self.along_x(j, side, 1 + side).wait_recv()
-                        self.half_on(j, side, 1 + side).start()
 
     def from_sibling(self, k):
         for j in self.ring_rows(k):
@@ -302,11 +297,15 @@
                 self.give(j, mine=False).wait_recv()
 
     def late(self, t):
+        for j in self.ring_rows(t - 2):
+            @pl.when(self.spreads(j))
+            def _(j=j):
+                for side in range(2):
+                    self.half_on(j, side, 3).wait_recv()
+
         @pl.when(self.place.core == 0)
         def _():
             if t == 2:
-                for side in range(2):
-                    self.half_on(0, side, 3).wait_recv()
                 for direction in range(2):
                     @pl.when(self.goes(direction, 1))
                     def _(direction=direction):
@@ -316,11 +315,6 @@
         for j in self.ring_rows(t - 2):
             @pl.when(self.needed(j))
             def _(j=j):
-                @pl.when(self.place.core == 1)
-                def _():
-                    for side in range(2):
-                        self.half_on(j, side, 3).wait_recv()
-
                 self.give(j).start()
 
     def run(self, queries_here):
@@ -373,38 +367,31 @@
 
     def drain(self):
         far = self.far
-        for side in range(2):
-            self.along_x(0, side, 0).wait_send()
-            self.half_on(0, side, 1 + side).wait_send()
         for j in range(2 * far):
             @pl.when(self.needed(j))
             def _(j=j):
                 self.give(j).wait_send()
 
-                @pl.when((self.place.core == 1) & (j > 0))
-                def _():
-                    for side in range(2):
-                        self.along_x(j, side, 0).wait_send()
-                        self.half_on(j, side, 1 + side).wait_send()
+            @pl.when(self.spreads(j))
+            def _(j=j):
+                for side in range(2):
+                    self.along_x(j, side, 0).wait_send()
+                    self.half_on(j, side, 1 + side).wait_send()
 
         for side in range(2):
             for k in range(1, far + 1):
                 @pl.when(self.goes(side, k))
                 def _(side=side, k=k):
                     j = 0 if k == 1 else 2 * k - 3 + side
-
-                    @pl.when(self.place.core == 0)
-                    def _():
-                        for i in range(4):
-                            if k < far or i // 2 == side:
+                    if k == far:
+                        self.half_along_z(j, side).wait_send()
+                    else:
+                        self.along_z(j, side, 0, k).wait_send()
+
+                        @pl.when(self.place.core == 0)
+                        def _():
+                            for i in range(1, 4):
                                 self.along_z(j, side, i, k).wait_send()
-
-                    @pl.when(self.place.core == 1)
-                    def _():
-                        if k < far:
-                            self.along_z(j, side, 0, k).wait_send()
-                        else:
-                            self.half_along_z(j, side).wait_send()
 
 
 def prefill(

time: 97.9 us -> 98.5 us (level)
  no operation moved by 1% of the time
where the time goes in v6:
time: 98.5 us; the launch traced here: 98.4 us
  Pallas kernels  96.7 us (98%)
  local copies, waits for them, and re-layouts  1.67 us (2%)
    pallas_call x1, Pallas kernels, prefill(): pl.pallas_call(kernel, out_shape=jax.ShapeDtypeStruct((rows, query_width)...  96.7 us

profile of v6, /device:TPU:249, one launch (start us, length us, event | category | flops | bytes accessed | tf_op | source)
XLA Modules:
  0.0 98.4 jit_solution(17431951225369971357)
XLA Ops:
  0.0 96.7 %prefill.1 = bf16[256,512]{1,0:T(8,128)(2,1)} custom-call(bf16[112,1280]{1,0:T(8,128)(2,1)} %bitcast.5, f32[1280]{0:T(1024)} %g_ref.1, bf16[320,5120]{1,0:T(8,128)(2,1)} %bitcast.4, f32[320]{0:T(512)} %ub_ref.1, bf16[320,4096]{1,0:T(8,128)(2,1)} %down_hbm.1, f32[512]{0:T(512)} %db_ref.1, bf16[256,512]{1,0:T(8,128)(2,1)} %text_ref.1, s32[16,32]{1,0:T(8,128)} %bitcast.6, ...), custom_call_target="tpu_custom_call" | custom-call | tf_op jit(solution)/shard_map/prefill/pallas_call | solution.py:750
  96.7 1.7 %copy.15 = bf16[256,512]{1,0:T(8,128)(2,1)} copy(bf16[256,512]{1,0:T(8,128)(2,1)} %prefill.1) | data formatting | bytes 524288

commit v7 on v6

--- a/solution.py
+++ b/solution.py
@@ -128,7 +128,7 @@
         self.half = kv.shape[3]
         self.rows = 2 * self.half
         self.heads = q3.shape[0]
-        self.together = min(2, self.heads)
+        self.together = 1
         self.group = self.together * self.rows
 
     def along_x(self, j, side, i):

time: 98.5 us -> 99 us (level)
  no operation moved by 1% of the time
where the time goes in v7:
time: 99 us; the launch traced here: 98.8 us
  Pallas kernels  97.2 us (98%)
  local copies, waits for them, and re-layouts  1.67 us (2%)
    pallas_call x1, Pallas kernels, prefill(): pl.pallas_call(kernel, out_shape=jax.ShapeDtypeStruct((rows, query_width)...  97.2 us

profile of v7, /device:TPU:249, one launch (start us, length us, event | category | flops | bytes accessed | tf_op | source)
XLA Modules:
  0.0 98.8 jit_solution(847262032928127455)
XLA Ops:
  0.0 97.2 %prefill.1 = bf16[256,512]{1,0:T(8,128)(2,1)} custom-call(bf16[112,1280]{1,0:T(8,128)(2,1)} %bitcast.5, f32[1280]{0:T(1024)} %g_ref.1, bf16[320,5120]{1,0:T(8,128)(2,1)} %bitcast.4, f32[320]{0:T(512)} %ub_ref.1, bf16[320,4096]{1,0:T(8,128)(2,1)} %down_hbm.1, f32[512]{0:T(512)} %db_ref.1, bf16[256,512]{1,0:T(8,128)(2,1)} %text_ref.1, s32[16,32]{1,0:T(8,128)} %bitcast.6, ...), custom_call_target="tpu_custom_call" | custom-call | tf_op jit(solution)/shard_map/prefill/pallas_call | solution.py:750
  97.2 1.7 %copy.15 = bf16[256,512]{1,0:T(8,128)(2,1)} copy(bf16[256,512]{1,0:T(8,128)(2,1)} %prefill.1) | data formatting | bytes 524288

commit v8 on v6

--- a/solution.py
+++ b/solution.py
@@ -190,11 +190,12 @@
             def _(side=side):
                 self.along_z(0, side, 0, 1).start()
 
-    def compute(self, row, c, restrict=None):
-        block = self.kv[row, c]
-        high = jnp.concatenate([block[i, :, :HD] for i in range(self.nx)], axis=1)
-        low = jnp.concatenate([block[i, :, HD : 2 * HD] for i in range(self.nx)], axis=1)
-        v = block[:, :, 2 * HD :].reshape(self.nx * self.half, HD)
+    def compute(self, rows, c, restrict=None):
+        blocks = [self.kv[row, c] for row in rows]
+        pieces = len(rows) * self.nx
+        high = jnp.concatenate([block[i, :, :HD] for block in blocks for i in range(self.nx)], axis=1)
+        low = jnp.concatenate([block[i, :, HD : 2 * HD] for block in blocks for i in range(self.nx)], axis=1)
+        v = jnp.concatenate([block[:, :, 2 * HD :].reshape(self.nx * self.half, HD) for block in blocks], axis=0)
         stacked = jnp.concatenate([high, low, high], axis=0)
         queries = [
             self.q3[h : h + self.together].reshape(self.group, 3 * HD) for h in range(0, self.heads, self.together)
@@ -203,11 +204,11 @@
         for i, score in enumerate(scores):
             at = slice(i * self.group, (i + 1) * self.group)
             if restrict is not None:
-                score = jnp.concatenate([restrict(n, score[:, n * HD : (n + 1) * HD]) for n in range(self.nx)], axis=1)
+                score = jnp.concatenate([restrict(n, score[:, n * HD : (n + 1) * HD]) for n in range(pieces)], axis=1)
             new = jnp.maximum(self.mx[at], jnp.max(score, axis=1, keepdims=True))
-            weights = jnp.exp2(score - jnp.concatenate([new] * self.nx, axis=1))
+            weights = jnp.exp2(score - jnp.concatenate([new] * pieces, axis=1))
             summed = weights[:, :HD]
-            for n in range(1, self.nx):
+            for n in range(1, pieces):
                 summed = summed + weights[:, n * HD : (n + 1) * HD]
             product = jnp.dot(weights.astype(jnp.bfloat16), v, preferred_element_type=jnp.float32)
             factor = jnp.exp2(self.mx[at] - new)
@@ -225,7 +226,7 @@
             limit = jnp.where(x > i, 2 * self.rows, jnp.where(x == i, 0, -2 * self.rows)) - c * self.half
             return jnp.where(ahead <= limit, piece, NEG)
 
-        self.compute(self.place.z, c, restrict)
+        self.compute([self.place.z], c, restrict)
 
     def pass_rows(self, k, chosen):
         if not 1 <= k < self.far:
@@ -347,16 +348,17 @@
             k = lax.div(i, 2) - 2 + odd
             c = jnp.where(odd == 1, core, 1 - core)
 
-            def attend(n, inner):
-                row = wrap(z + k * (2 * n - 1), nz)
-
-                @pl.when((k >= 1) & (k <= far) & (row < z) & ((k < far) | (n == 0)))
-                def _():
-                    self.compute(row, c)
-
-                return inner
-
-            lax.fori_loop(0, 2, attend, 0)
+            below, above = wrap(z - k, nz), wrap(z + k, nz)
+            reached = (k >= 1) & (k <= far)
+
+            @pl.when(reached & (k < far) & (below < z) & (above < z))
+            def _():
+                self.compute([below, above], c)
+
+            @pl.when(reached & (below < z) & ((k == far) | (above >= z)))
+            def _():
+                self.compute([below], c)
+
             return carry
 
         lax.fori_loop(0, 2 * (far + 3), phase, 0)

time: 98.5 us -> 97.5 us (0.990)
  Pallas kernels: 96.7 us -> 95.7 us
    pallas_call x1, Pallas kernels: 96.7 us -> 95.7 us  [prefill(): pl.pallas_call(kernel, out_shape=jax.ShapeDtypeStruct((rows, query_width)...]
where the time goes in v8:
time: 97.5 us; the launch traced here: 97.4 us
  Pallas kernels  95.7 us (98%)
  local copies, waits for them, and re-layouts  1.67 us (2%)
    pallas_call x1, Pallas kernels, prefill(): pl.pallas_call(kernel, out_shape=jax.ShapeDtypeStruct((rows, query_width)...  95.7 us

profile of v8, /device:TPU:249, one launch (start us, length us, event | category | flops | bytes accessed | tf_op | source)
XLA Modules:
  0.0 97.4 jit_solution(5088255660005036718)
XLA Ops:
  0.0 95.7 %prefill.1 = bf16[256,512]{1,0:T(8,128)(2,1)} custom-call(bf16[112,1280]{1,0:T(8,128)(2,1)} %bitcast.5, f32[1280]{0:T(1024)} %g_ref.1, bf16[320,5120]{1,0:T(8,128)(2,1)} %bitcast.4, f32[320]{0:T(512)} %ub_ref.1, bf16[320,4096]{1,0:T(8,128)(2,1)} %down_hbm.1, f32[512]{0:T(512)} %db_ref.1, bf16[256,512]{1,0:T(8,128)(2,1)} %text_ref.1, s32[16,32]{1,0:T(8,128)} %bitcast.6, ...), custom_call_target="tpu_custom_call" | custom-call | tf_op jit(solution)/shard_map/prefill/pallas_call | solution.py:752
  95.7 1.7 %copy.15 = bf16[256,512]{1,0:T(8,128)(2,1)} copy(bf16[256,512]{1,0:T(8,128)(2,1)} %prefill.1) | data formatting | bytes 524288
